TPU v7x, 32 devices: a whole 2x2x4 slice. The times are simulated.
32 devices in a mesh: grp: 4 (over x, core), cell: 8 (over z, y).
Axes of the slice: x: 2, y: 2, z: 4, core: 2. Of those that a mesh axis runs over, the one named last changes fastest.
Arguments:
- rhs: float32 [64, 2, 32, 16, 128], P('grp', None, 'cell'), may hold values from -8 to 8
- log_perm: float32 [64, 32, 16, 128], P('grp', 'cell'), may hold values from -1.5 to 1.5
- porosity: float32 [64, 32, 16, 128], P('grp', 'cell'), may hold values from 0.1 to 0.3
- saturation: float32 [64, 32, 16, 128], P('grp', 'cell'), may hold values from 0.2 to 0.8
- pressure: float32 [64, 32, 16, 128], P('grp', 'cell'), may hold values from -6 to 6
- obs_values: float32 [256], replicated, may hold values from -6 to 6
- obs_error: float32 [256], replicated, may hold values from 0.1 to 1
- noise: float32 [64, 256], replicated, may hold values from -6 to 6
- well_cell: int32 [128], replicated, may hold values from 0 to 65535
- obs_well: int32 [256], replicated, may hold values from 0 to 127
Outputs:
- increment: float32 [64, 2, 32, 16, 128], P('grp', None, 'cell')
- log_perm_post: float32 [64, 32, 16, 128], P('grp', 'cell')
- porosity_post: float32 [64, 32, 16, 128], P('grp', 'cell')
All inputs are finite; a program needn't handle non-finite values.
Results may differ from a plain program's by a relative error of at most 0.0003.
Values sent between devices are 32-bit elements; how exact they have to be, the bound alone decides.
A program may use at most 128 MiB of HBM per device.

v0:
```python
import math

import jax
import jax.numpy as jnp
from jax import lax
from jax.sharding import PartitionSpec as P

KRYLOV = 4


epsilon = 1e-06
time_step = 0.1
compress = 0.5
inflation = 4.0


def with_halo(block, sides, width):
    for axis, dim in sides:
        count = lax.axis_size(axis)
        forward = [(i, i + 1) for i in range(count - 1)]
        backward = [(target, source) for source, target in forward]
        low = lax.ppermute(
            lax.slice_in_dim(block, block.shape[dim] - width, None, axis=dim), axis, forward
        )
        high = lax.ppermute(lax.slice_in_dim(block, 0, width, axis=dim), axis, backward)
        block = jnp.concatenate([low, block, high], axis=dim)
    return block


def mobility(sat_field):
    return sat_field * sat_field + 0.5 * (1.0 - sat_field) * (1.0 - sat_field)


def face_pair(perm_low, perm_high, sat_low, sat_high):
    trans = (
        2.0
        * perm_low
        * perm_high
        / (perm_low + perm_high)
        * (0.5 * (mobility(sat_low) + mobility(sat_high)))
    )
    return (trans, trans * (0.5 * (sat_low + sat_high)))


def plane_faces(perm, sat_field):
    plane_rows = perm.shape[-2]
    plane_cols = perm.shape[-1]
    keep_rows = (
        lax.broadcasted_iota(jnp.int32, (plane_rows, plane_cols), 0) < plane_rows - 1
    ).astype(jnp.float32)
    keep_cols = (
        lax.broadcasted_iota(jnp.int32, (plane_rows, plane_cols), 1) < plane_cols - 1
    ).astype(jnp.float32)
    trans_y, frac_y = face_pair(
        perm, jnp.roll(perm, -1, -2), sat_field, jnp.roll(sat_field, -1, -2)
    )
    trans_z, frac_z = face_pair(
        perm, jnp.roll(perm, -1, -1), sat_field, jnp.roll(sat_field, -1, -1)
    )
    return (trans_y * keep_rows, frac_y * keep_rows, trans_z * keep_cols, frac_z * keep_cols)


def operator(padded, second, coeffs):
    accum, trans_x, frac_x, trans_y, frac_y, trans_z, frac_z = coeffs
    first = padded[..., 1:-1, :, :]
    diff_x = padded[..., 1:, :, :] - padded[..., :-1, :, :]
    diff_y = jnp.roll(first, -1, -2) - first
    diff_z = jnp.roll(first, -1, -1) - first

    def net(coef_x, coef_y, coef_z):
        flow_x = coef_x * diff_x
        flow_y = coef_y * diff_y
        flow_z = coef_z * diff_z
        return (
            flow_x[..., :-1, :, :]
            - flow_x[..., 1:, :, :]
            + (jnp.roll(flow_y, 1, -2) - flow_y)
            + (jnp.roll(flow_z, 1, -1) - flow_z)
        )

    out_pressure = accum * (compress * first + 0.5 * second) + net(trans_x, trans_y, trans_z)
    out_water = accum * second + net(frac_x, frac_y, frac_z)
    return (out_pressure, out_water)


def least_squares(columns, beta):
    rows = [list(column) for column in columns]
    cosines = []
    sines = []
    target = [beta] + [jnp.zeros_like(beta) for column in columns]
    for jdx in range(len(rows)):
        column = rows[jdx]
        for idx in range(jdx):
            upper = cosines[idx] * column[idx] + sines[idx] * column[idx + 1]
            column[idx + 1] = -sines[idx] * column[idx] + cosines[idx] * column[idx + 1]
            column[idx] = upper
        radius = jnp.sqrt(column[jdx] * column[jdx] + column[jdx + 1] * column[jdx + 1])
        cosines.append(column[jdx] / radius)
        sines.append(column[jdx + 1] / radius)
        column[jdx] = radius
        target[jdx + 1] = -sines[jdx] * target[jdx]
        target[jdx] = cosines[jdx] * target[jdx]
    count = len(rows)
    solved = [None] * count
    for jdx in reversed(range(count)):
        partial_sum = target[jdx]
        for idx in range(jdx + 1, count):
            partial_sum = partial_sum - rows[idx][jdx] * solved[idx]
        solved[jdx] = partial_sum / rows[jdx][jdx]
    return solved


def ensemble_weights(predicted, obs_values, obs_error, noise):
    members = predicted.shape[0]
    sigma = math.sqrt(inflation) * obs_error
    center = jnp.mean(predicted, axis=0)
    spread = (predicted - center) / (math.sqrt(members - 1.0) * sigma)
    innov = (obs_values + sigma * noise - predicted) / sigma
    gram = jnp.eye(members, dtype=jnp.float32) + jnp.dot(
        spread, spread.T, precision=lax.Precision.HIGHEST, preferred_element_type=jnp.float32
    )
    cross = jnp.dot(
        spread, innov.T, precision=lax.Precision.HIGHEST, preferred_element_type=jnp.float32
    )
    factor = jnp.linalg.cholesky(gram)
    return jax.scipy.linalg.cho_solve((factor, True), cross)


def expand(values):
    return values[:, None, None, None, None]


def inner(left, right):
    return jnp.sum(left * right, axis=(1, 2, 3, 4))


def local(
    rhs, log_perm, porosity, saturation, pressure, obs_values, obs_error, noise, well_cell, obs_well
):
    local_members, slab_x, plane_rows, plane_cols = log_perm.shape
    members = noise.shape[0]
    plane = plane_rows * plane_cols
    cells_dev = slab_x * plane
    slab_index = lax.axis_index("cell")
    slab_count = lax.axis_size("cell")
    stacked = jnp.stack([log_perm, saturation], axis=1)
    rimmed = with_halo(stacked, (("cell", 2),), 1)
    perm_pad = jnp.exp(rimmed[:, 0])
    sat_pad = rimmed[:, 1]
    trans_x, frac_x = face_pair(perm_pad[:, :-1], perm_pad[:, 1:], sat_pad[:, :-1], sat_pad[:, 1:])
    face_pos = lax.broadcasted_iota(jnp.int32, (slab_x + 1, 1, 1), 0)
    keep_face = jnp.where(
        face_pos == 0,
        slab_index > 0,
        jnp.where(face_pos == slab_x, slab_index < slab_count - 1, True),
    ).astype(jnp.float32)
    trans_x = trans_x * keep_face
    frac_x = frac_x * keep_face
    trans_y, frac_y, trans_z, frac_z = plane_faces(perm_pad[:, 1:-1], saturation)
    coeffs = (porosity / time_step, trans_x, frac_x, trans_y, frac_y, trans_z, frac_z)
    columns = []
    beta = jnp.sqrt(lax.psum(inner(rhs, rhs), "cell") + epsilon)
    basis = [rhs / expand(beta)]
    for jdx in range(KRYLOV):
        vector = basis[jdx]
        padded = with_halo(vector[:, 0], (("cell", 1),), 1)
        out_pressure, out_water = operator(padded, vector[:, 1], coeffs)
        image = jnp.stack([out_pressure, out_water], 1)
        local_dots = jnp.stack([inner(basis[idx], image) for idx in range(jdx + 1)], 0)
        projected = lax.psum(local_dots, "cell")
        for idx in range(jdx + 1):
            image = image - expand(projected[idx]) * basis[idx]
        height = jnp.sqrt(lax.psum(inner(image, image), "cell") + epsilon)
        columns.append([projected[idx] for idx in range(jdx + 1)] + [height])
        basis.append(image / expand(height))
    solved = least_squares(columns, beta)
    increment = expand(solved[0]) * basis[0]
    for jdx in range(1, KRYLOV):
        increment = increment + expand(solved[jdx]) * basis[jdx]
    flat = jnp.stack([pressure + increment[:, 0], saturation + increment[:, 1]], 1).reshape(
        local_members, 2 * cells_dev
    )
    cells = jnp.take(well_cell, obs_well)
    wells = well_cell.shape[0]
    component = (jnp.arange(obs_well.shape[0], dtype=jnp.int32) >= wells).astype(jnp.int32)
    slab_row = cells // plane - slab_index * slab_x
    inside = (slab_row >= 0) & (slab_row < slab_x)
    local_cell = jnp.where(inside, slab_row * plane + cells % plane, 0)
    picked = jnp.take(flat, component * cells_dev + local_cell, axis=1) * inside.astype(jnp.float32)
    slab_pred = lax.psum(picked, "cell")
    predicted = lax.all_gather(slab_pred, "grp", axis=0, tiled=True)
    weights = ensemble_weights(predicted, obs_values, obs_error, noise)
    params = jnp.stack([log_perm, porosity], 1).reshape(local_members, 2 * cells_dev)
    offset = lax.axis_index("grp") * local_members
    scale_factor = 1.0 / math.sqrt(members - 1.0)
    scaled = params * scale_factor
    own_columns = lax.dynamic_slice_in_dim(weights, offset, local_members, 1)
    update = jnp.dot(
        own_columns.T,
        lax.all_gather(scaled, "grp", axis=0, tiled=True),
        precision=lax.Precision.HIGHEST,
        preferred_element_type=jnp.float32,
    )
    posterior = params + update
    posterior = posterior.reshape(local_members, 2, slab_x, plane_rows, plane_cols)
    return (increment, posterior[:, 0], posterior[:, 1])


def solution(mesh):
    in_specs = (
        P("grp", None, "cell", None, None),
        P("grp", "cell", None, None),
        P("grp", "cell", None, None),
        P("grp", "cell", None, None),
        P("grp", "cell", None, None),
        P(),
        P(),
        P(),
        P(),
        P(),
    )
    out_specs = (
        P("grp", None, "cell", None, None),
        P("grp", "cell", None, None),
        P("grp", "cell", None, None),
    )
    return jax.shard_map(local, mesh=mesh, in_specs=in_specs, out_specs=out_specs, check_vma=False)
```

profile of v0, /device:TPU:0, one launch (start us, length us, event | category | flops | bytes accessed | tf_op | source)
XLA Modules:
  0.0 337.8 jit_solution(16407738990363813492)
XLA Ops:
  7.2 2.0 fusion.61
  9.2 5.0 %collective-permute-start = (f32[16,2,1,16,128]{4,3,2,0,1:T(8,128)}, f32[16,2,1,16,128]{4,3,2,0,1:T(8,128)S(1)}, u32[]{:S(2)}, u32[]{:S(2)}) collective-permute-start(f32[16,2,1,16,128]{4,3,2,0,1:T(8,128)} %get-tuple-element.67), channel_id=1, source_target_pairs={{0,1},{1,2},{2,3},{3,4},{4,5},{5,6},{6,7},{8,9},{9,10},{10,11},{11... | collective-permute-start | bytes 786440 | tf_op jit(solution)/shard_map/ppermute | solution.py:22
  14.5 1.3 collective-permute-start.1
  15.8 23.5 %psum.70 = f32[16]{0:T(128)S(1)} all-reduce(f32[16]{0:T(128)S(1)} %multiply_reduce_fusion.14), channel_id=1, replica_groups=mesh['grp'=4,'cell'=8] {'cell'}, use_global_device_ids=true, to_apply=%region_1.2 | all-reduce | flops 16 | bytes 128 | tf_op jit(solution)/shard_map/psum | solution.py:162
  40.1 1.3 collective-permute-start.2
  41.4 5.2 %collective-permute-start.3 = (f32[16,1,16,128]{3,2,1,0:T(8,128)}, f32[16,1,16,128]{3,2,1,0:T(8,128)}, u32[]{:S(2)}, u32[]{:S(2)}) collective-permute-start(f32[16,1,16,128]{3,2,1,0:T(8,128)} %get-tuple-element.82), channel_id=1, source_target_pairs={{0,1},{1,2},{2,3},{3,4},{4,5},{5,6},{6,7},{8,9},{9,10},{10,11},{11... | collective-permute-start | bytes 393224 | tf_op jit(solution)/shard_map/ppermute | solution.py:22
  46.8 1.0 copy-done.22
  47.8 1.7 bitcast_multiply_fusion
  49.6 1.9 gather_fusion
  51.6 0.8 slice.516
  52.4 1.0 slice.522
  53.4 0.8 slice.402
  54.3 1.0 slice.410
  55.3 1.2 pad_maximum_fusion
  58.2 1.1 multiply_multiply_fusion.11
  59.3 1.6 fusion.100
  61.4 2.6 fusion.60
  66.2 18.1 %psum.71 = f32[16]{0:T(128)S(1)} all-reduce(f32[16]{0:T(128)S(1)} %multiply_reduce_fusion.13), channel_id=1, replica_groups=mesh['grp'=4,'cell'=8] {'cell'}, use_global_device_ids=true, to_apply=%region_3.4 | all-reduce | flops 16 | bytes 128 | tf_op jit(solution)/shard_map/psum | solution.py:170
  84.3 1.6 multiply_reduce_fusion.12
  85.9 18.1 %psum.72 = f32[16]{0:T(128)S(1)} all-reduce(f32[16]{0:T(128)S(1)} %get-tuple-element.23), channel_id=1, replica_groups=mesh['grp'=4,'cell'=8] {'cell'}, use_global_device_ids=true, to_apply=%region_5.6 | all-reduce | flops 16 | bytes 128 | tf_op jit(solution)/shard_map/psum | solution.py:173
  104.5 1.4 collective-permute-start.4
  105.9 4.6 %collective-permute-start.5 = (f32[16,1,16,128]{3,2,1,0:T(8,128)S(1)}, f32[16,1,16,128]{3,2,1,0:T(8,128)S(1)}, u32[]{:S(2)}, u32[]{:S(2)}) collective-permute-start(f32[16,1,16,128]{3,2,1,0:T(8,128)S(1)} %get-tuple-element.80), channel_id=1, source_target_pairs={{0,1},{1,2},{2,3},{3,4},{4,5},{5,6},{6,7},{8,9},{9,10},{10,11},{11... | collective-permute-start | bytes 393224 | tf_op jit(solution)/shard_map/ppermute | solution.py:22
  111.6 1.4 collective-permute-done.5
  115.5 19.6 %psum.73 = f32[2,16]{1,0:T(2,128)S(1)} all-reduce(f32[2,16]{1,0:T(2,128)S(1)} %pad_maximum_fusion.14), channel_id=1, replica_groups=mesh['grp'=4,'cell'=8] {'cell'}, use_global_device_ids=true, to_apply=%region_8.9 | all-reduce | flops 32 | bytes 256 | tf_op jit(solution)/shard_map/psum | solution.py:170
  135.1 1.7 multiply_reduce_fusion.9
  136.7 17.2 %psum.74 = f32[16]{0:T(128)S(1)} all-reduce(f32[16]{0:T(128)S(1)} %get-tuple-element.21), channel_id=1, replica_groups=mesh['grp'=4,'cell'=8] {'cell'}, use_global_device_ids=true, to_apply=%region_10.11 | all-reduce | flops 16 | bytes 128 | tf_op jit(solution)/shard_map/psum | solution.py:173
  154.4 1.4 collective-permute-start.6
  155.9 4.7 %collective-permute-start.7 = (f32[16,1,16,128]{3,2,1,0:T(8,128)S(1)}, f32[16,1,16,128]{3,2,1,0:T(8,128)S(1)}, u32[]{:S(2)}, u32[]{:S(2)}) collective-permute-start(f32[16,1,16,128]{3,2,1,0:T(8,128)S(1)} %get-tuple-element.78), channel_id=1, source_target_pairs={{0,1},{1,2},{2,3},{3,4},{4,5},{5,6},{6,7},{8,9},{9,10},{10,11},{11... | collective-permute-start | bytes 393224 | tf_op jit(solution)/shard_map/ppermute | solution.py:22
  161.8 1.4 collective-permute-done.7
  165.6 19.7 %psum.75 = f32[3,16]{1,0:T(4,128)S(1)} all-reduce(f32[3,16]{1,0:T(4,128)S(1)} %pad_maximum_fusion.12), channel_id=1, replica_groups=mesh['grp'=4,'cell'=8] {'cell'}, use_global_device_ids=true, to_apply=%region_14.15 | all-reduce | flops 48 | bytes 384 | tf_op jit(solution)/shard_map/psum | solution.py:170
  185.3 2.7 multiply_reduce_fusion.5
  187.9 17.8 %psum.76 = f32[16]{0:T(128)S(1)} all-reduce(f32[16]{0:T(128)S(1)} %get-tuple-element.19), channel_id=1, replica_groups=mesh['grp'=4,'cell'=8] {'cell'}, use_global_device_ids=true, to_apply=%region_16.17 | all-reduce | flops 16 | bytes 128 | tf_op jit(solution)/shard_map/psum | solution.py:173
  205.7 1.4 copy_divide_fusion
  207.5 1.4 collective-permute-start.8
  208.9 4.6 %collective-permute-start.9 = (f32[16,1,16,128]{3,2,1,0:T(8,128)S(1)}, f32[16,1,16,128]{3,2,1,0:T(8,128)S(1)}, u32[]{:S(2)}, u32[]{:S(2)}) collective-permute-start(f32[16,1,16,128]{3,2,1,0:T(8,128)S(1)} %get-tuple-element.76), channel_id=1, source_target_pairs={{0,1},{1,2},{2,3},{3,4},{4,5},{5,6},{6,7},{8,9},{9,10},{10,11},{11... | collective-permute-start | bytes 393224 | tf_op jit(solution)/shard_map/ppermute | solution.py:22
  214.7 1.4 collective-permute-done.9
  219.0 19.6 %psum.77 = f32[4,16]{1,0:T(4,128)S(1)} all-reduce(f32[4,16]{1,0:T(4,128)S(1)} %pad_maximum_fusion.13), channel_id=1, replica_groups=mesh['grp'=4,'cell'=8] {'cell'}, use_global_device_ids=true, to_apply=%region_21.22 | all-reduce | flops 64 | bytes 512 | tf_op jit(solution)/shard_map/psum | solution.py:170
  238.6 2.2 multiply_reduce_fusion
  240.8 17.6 %psum.78 = f32[16]{0:T(128)S(1)} all-reduce(f32[16]{0:T(128)S(1)} %multiply_reduce_fusion), channel_id=1, replica_groups=mesh['grp'=4,'cell'=8] {'cell'}, use_global_device_ids=true, to_apply=%region_23.24 | all-reduce | flops 16 | bytes 128 | tf_op jit(solution)/shard_map/psum | solution.py:173
  258.5 1.8 multiply_add_fusion
  261.5 4.6 %copy.101 = f32[16,2,4,16,128]{0,4,3,2,1:T(8,128)} copy(f32[16,2,4,16,128]{4,3,2,0,1:T(8,128)S(1)} %pad_maximum_fusion.6) | data formatting | bytes 2097152 | tf_op jit(solution)/shard_map/stack | solution.py:180
  266.1 4.2 %gather_fusion.1 = f32[256,16]{1,0:T(8,128)S(1)} fusion(f32[16,16384]{0,1:T(8,128)} %bitcast.329, s32[1024]{0:T(1024)S(1)} %pad_clamp_fusion), kind=kCustom, calls=%fused_computation.1 | custom fusion | bytes 33792 | tf_op jit(solution)/shard_map/jit(_take)/gather | solution.py:189
  270.4 35.7 %psum.79 = f32[16,256]{0,1:T(8,128)S(1)} all-reduce(f32[16,256]{0,1:T(8,128)S(1)} %multiply_bitcast_fusion), channel_id=1, replica_groups=mesh['grp'=4,'cell'=8] {'cell'}, use_global_device_ids=true, to_apply=%region_24.25 | all-reduce | flops 4096 | bytes 32768 | tf_op jit(solution)/shard_map/psum | solution.py:190
  306.2 5.5 %all_gather.6 = f32[64,256]{1,0:T(8,128)S(1)} all-gather(f32[16,256]{1,0:T(8,128)S(1)} %copy.102), channel_id=1, replica_groups=mesh['grp'=4,'cell'=8] {'grp'}, dimensions={0}, use_global_device_ids=true | all-gather | bytes 81920 | tf_op jit(solution)/shard_map/all_gather | solution.py:191
  312.1 5.8 %cholesky.17 = f32[64,64]{1,0:T(8,128)S(1)} custom-call(f32[64,64]{1,0:T(8,128)S(1)} %fusion.78), custom_call_target="Cholesky" | custom-call | tf_op jit(solution)/shard_map/jit(cholesky)/cholesky | solution.py:125
  319.2 4.9 %custom-call.10 = f32[1,64,64]{1,2,0:T(8,128)S(1)} custom-call(f32[1,64,64]{2,1,0:T(8,128)S(1)} %fusion.72), custom_call_target="InvertDiagBlocksLowerTriangular" | custom-call | tf_op jit(solution)/shard_map/jit(_cho_solve)/triangular_solve | solution.py:126
  324.9 4.7 %fusion = f32[2,8,128,128]{3,1,2,0:T(8,128)S(1)} fusion(f32[64,16384]{1,0:T(8,128)} %all-gather.2.cloned.1.call-done, f32[2,8,128,128]{3,2,1,0:T(8,128)S(1)} %bitcast.328, f32[64,64]{0,1:T(8,128)S(1)} %fusion.73, s32[]{:T(128)S(6)} %select_n.96), kind=kOutput, calls=%fused_computation.4 | convolution fusion | flops 201588736 | bytes 6299652 | tf_op jit(solution)/shard_map/dot_general | solution.py:198
  329.8 1.1 slice_bitcast_fusion.1
  (204 shorter events, 21.7 us)
Async XLA Ops:
  7.2 42.4 %copy-start = (s32[128]{0:T(128)S(1)}, s32[128]{0:T(128)}, u32[]{:S(2)}) copy-start(s32[128]{0:T(128)} %param.18) | copy-start | bytes 1540
  7.2 7.1 %copy-start.2 = (f32[16,2,4,16,128]{4,3,2,1,0:T(8,128)S(1)}, f32[16,2,4,16,128]{4,3,2,1,0:T(8,128)}, u32[]{:S(2)}) copy-start(f32[16,2,4,16,128]{4,3,2,1,0:T(8,128)} %param.10) | copy-start | bytes 3145732
  7.2 317.7 %all-gather.2.cloned.1.call-start = ((), (), s32[]{:S(2)}) async-start(), calls=%async_computation | async-start | bytes 5242880 | tf_op jit(solution)/shard_map/all_gather | solution.py:200
  9.2 37.4 %copy-start.5 = (f32[16,4,16,128]{3,2,1,0:T(8,128)S(1)}, f32[16,4,16,128]{3,2,1,0:T(8,128)}, u32[]{:S(2)}) copy-start(f32[16,4,16,128]{3,2,1,0:T(8,128)} %param.12) | copy-start | bytes 1572868
  9.2 37.4 %copy-start.37 = (f32[16,4,16,128]{3,2,1,0:T(8,128)S(1)}, f32[16,4,16,128]{3,2,1,0:T(8,128)}, u32[]{:S(2)}) copy-start(f32[16,4,16,128]{3,2,1,0:T(8,128)} %param.11) | copy-start | bytes 1572868
  9.2 46.1 %collective-permute-start = (f32[16,2,1,16,128]{4,3,2,0,1:T(8,128)}, f32[16,2,1,16,128]{4,3,2,0,1:T(8,128)S(1)}, u32[]{:S(2)}, u32[]{:S(2)}) collective-permute-start(f32[16,2,1,16,128]{4,3,2,0,1:T(8,128)} %get-tuple-element.67), channel_id=1, source_target_pairs={{0,1},{1,2},{2,3},{3,4},{4,5},{5,6},{6,7},{8,9},{9,10},{10,11},{11... | collective-permute-start | bytes 786440 | tf_op jit(solution)/shard_map/ppermute | solution.py:22
  14.5 40.8 %collective-permute-start.1 = (f32[16,2,1,16,128]{4,3,2,0,1:T(8,128)}, f32[16,2,1,16,128]{4,3,2,0,1:T(8,128)}, u32[]{:S(2)}, u32[]{:S(2)}) collective-permute-start(f32[16,2,1,16,128]{4,3,2,0,1:T(8,128)} %get-tuple-element.68), channel_id=1, source_target_pairs={{1,0},{2,1},{3,2},{4,3},{5,4},{6,5},{7,6},{9,8},{10,9},{11,10},{12... | collective-permute-start | bytes 786440 | tf_op jit(solution)/shard_map/ppermute | solution.py:25
  40.1 21.3 %collective-permute-start.2 = (f32[16,1,16,128]{3,2,1,0:T(8,128)}, f32[16,1,16,128]{3,2,1,0:T(8,128)}, u32[]{:S(2)}, u32[]{:S(2)}) collective-permute-start(f32[16,1,16,128]{3,2,1,0:T(8,128)} %get-tuple-element.81), channel_id=1, source_target_pairs={{1,0},{2,1},{3,2},{4,3},{5,4},{6,5},{7,6},{9,8},{10,9},{11,10},{12... | collective-permute-start | bytes 393224 | tf_op jit(solution)/shard_map/ppermute | solution.py:25
  41.4 20.0 %collective-permute-start.3 = (f32[16,1,16,128]{3,2,1,0:T(8,128)}, f32[16,1,16,128]{3,2,1,0:T(8,128)}, u32[]{:S(2)}, u32[]{:S(2)}) collective-permute-start(f32[16,1,16,128]{3,2,1,0:T(8,128)} %get-tuple-element.82), channel_id=1, source_target_pairs={{0,1},{1,2},{2,3},{3,4},{4,5},{5,6},{6,7},{8,9},{9,10},{10,11},{11... | collective-permute-start | bytes 393224 | tf_op jit(solution)/shard_map/ppermute | solution.py:22
  47.8 1.7 copy-start.45
  49.6 3.8 %copy-start.3 = (f32[16,4,16,128]{3,2,1,0:T(8,128)S(1)}, f32[16,4,16,128]{3,2,1,0:T(8,128)}, u32[]{:S(2)}) copy-start(f32[16,4,16,128]{3,2,1,0:T(8,128)} %param.13) | copy-start | bytes 1572868
  52.4 2.9 copy-start.46
  56.7 1.3 copy-start.33
  56.7 1.5 copy-start.34
  59.3 1.6 copy-start.12
  59.3 51.2 %copy-start.9 = (f32[16,4,16,128]{3,2,1,0:T(8,128)}, f32[16,4,16,128]{3,2,1,0:T(8,128)S(1)}, u32[]{:S(2)}) copy-start(f32[16,4,16,128]{3,2,1,0:T(8,128)S(1)} %get-tuple-element.26) | copy-start | bytes 1572868
  104.2 6.3 %copy-start.13 = (f32[16,4,16,128]{3,2,1,0:T(8,128)S(1)}, f32[16,4,16,128]{3,2,1,0:T(8,128)}, u32[]{:S(2)}) copy-start(f32[16,4,16,128]{3,2,1,0:T(8,128)} %copy-done.12) | copy-start | bytes 1572868
  104.2 6.3 %copy-start.24 = (f32[16,4,16,128]{3,2,1,0:T(8,128)S(1)}, f32[16,4,16,128]{3,2,1,0:T(8,128)}, u32[]{:S(2)}) copy-start(f32[16,4,16,128]{3,2,1,0:T(8,128)} %get-tuple-element.32) | copy-start | bytes 1572868
  104.2 6.3 %copy-start.27 = (f32[16,4,16,128]{3,2,1,0:T(8,128)S(1)}, f32[16,4,16,128]{3,2,1,0:T(8,128)}, u32[]{:S(2)}) copy-start(f32[16,4,16,128]{3,2,1,0:T(8,128)} %get-tuple-element.54) | copy-start | bytes 1572868
  104.5 7.1 %collective-permute-start.4 = (f32[16,1,16,128]{3,2,1,0:T(8,128)S(1)}, f32[16,1,16,128]{3,2,1,0:T(8,128)S(1)}, u32[]{:S(2)}, u32[]{:S(2)}) collective-permute-start(f32[16,1,16,128]{3,2,1,0:T(8,128)S(1)} %get-tuple-element.79), channel_id=1, source_target_pairs={{1,0},{2,1},{3,2},{4,3},{5,4},{6,5},{7,6},{9,8},{10,9},{11,10},{12... | collective-permute-start | bytes 393224 | tf_op jit(solution)/shard_map/ppermute | solution.py:25
  105.9 7.1 %collective-permute-start.5 = (f32[16,1,16,128]{3,2,1,0:T(8,128)S(1)}, f32[16,1,16,128]{3,2,1,0:T(8,128)S(1)}, u32[]{:S(2)}, u32[]{:S(2)}) collective-permute-start(f32[16,1,16,128]{3,2,1,0:T(8,128)S(1)} %get-tuple-element.80), channel_id=1, source_target_pairs={{0,1},{1,2},{2,3},{3,4},{4,5},{5,6},{6,7},{8,9},{9,10},{10,11},{11... | collective-permute-start | bytes 393224 | tf_op jit(solution)/shard_map/ppermute | solution.py:22
  111.1 1.9 copy-start.16
  111.1 1.9 copy-start.19
  154.1 6.5 %copy-start.10 = (f32[16,4,16,128]{3,2,1,0:T(8,128)S(1)}, f32[16,4,16,128]{3,2,1,0:T(8,128)}, u32[]{:S(2)}) copy-start(f32[16,4,16,128]{3,2,1,0:T(8,128)} %copy-done.9) | copy-start | bytes 1572868
  154.1 6.5 %copy-start.14 = (f32[16,4,16,128]{3,2,1,0:T(8,128)S(1)}, f32[16,4,16,128]{3,2,1,0:T(8,128)}, u32[]{:S(2)}) copy-start(f32[16,4,16,128]{3,2,1,0:T(8,128)} %copy-done.12) | copy-start | bytes 1572868
  154.1 6.5 %copy-start.25 = (f32[16,4,16,128]{3,2,1,0:T(8,128)S(1)}, f32[16,4,16,128]{3,2,1,0:T(8,128)}, u32[]{:S(2)}) copy-start(f32[16,4,16,128]{3,2,1,0:T(8,128)} %get-tuple-element.32) | copy-start | bytes 1572868
  154.1 6.5 %copy-start.28 = (f32[16,4,16,128]{3,2,1,0:T(8,128)S(1)}, f32[16,4,16,128]{3,2,1,0:T(8,128)}, u32[]{:S(2)}) copy-start(f32[16,4,16,128]{3,2,1,0:T(8,128)} %get-tuple-element.54) | copy-start | bytes 1572868
  154.4 7.3 %collective-permute-start.6 = (f32[16,1,16,128]{3,2,1,0:T(8,128)S(1)}, f32[16,1,16,128]{3,2,1,0:T(8,128)S(1)}, u32[]{:S(2)}, u32[]{:S(2)}) collective-permute-start(f32[16,1,16,128]{3,2,1,0:T(8,128)S(1)} %get-tuple-element.77), channel_id=1, source_target_pairs={{1,0},{2,1},{3,2},{4,3},{5,4},{6,5},{7,6},{9,8},{10,9},{11,10},{12... | collective-permute-start | bytes 393224 | tf_op jit(solution)/shard_map/ppermute | solution.py:25
  155.9 7.3 %collective-permute-start.7 = (f32[16,1,16,128]{3,2,1,0:T(8,128)S(1)}, f32[16,1,16,128]{3,2,1,0:T(8,128)S(1)}, u32[]{:S(2)}, u32[]{:S(2)}) collective-permute-start(f32[16,1,16,128]{3,2,1,0:T(8,128)S(1)} %get-tuple-element.78), channel_id=1, source_target_pairs={{0,1},{1,2},{2,3},{3,4},{4,5},{5,6},{6,7},{8,9},{9,10},{10,11},{11... | collective-permute-start | bytes 393224 | tf_op jit(solution)/shard_map/ppermute | solution.py:22
  161.2 1.9 copy-start.17
  161.2 1.9 copy-start.20
  161.7 1.6 copy-start.6
  207.2 6.4 %copy-start.11 = (f32[16,4,16,128]{3,2,1,0:T(8,128)S(1)}, f32[16,4,16,128]{3,2,1,0:T(8,128)}, u32[]{:S(2)}) copy-start(f32[16,4,16,128]{3,2,1,0:T(8,128)} %copy-done.9) | copy-start | bytes 1572868
  207.2 6.4 %copy-start.15 = (f32[16,4,16,128]{3,2,1,0:T(8,128)S(1)}, f32[16,4,16,128]{3,2,1,0:T(8,128)}, u32[]{:S(2)}) copy-start(f32[16,4,16,128]{3,2,1,0:T(8,128)} %copy-done.12) | copy-start | bytes 1572868
  207.2 6.4 %copy-start.26 = (f32[16,4,16,128]{3,2,1,0:T(8,128)S(1)}, f32[16,4,16,128]{3,2,1,0:T(8,128)}, u32[]{:S(2)}) copy-start(f32[16,4,16,128]{3,2,1,0:T(8,128)} %get-tuple-element.32) | copy-start | bytes 1572868
  207.2 6.4 %copy-start.29 = (f32[16,4,16,128]{3,2,1,0:T(8,128)S(1)}, f32[16,4,16,128]{3,2,1,0:T(8,128)}, u32[]{:S(2)}) copy-start(f32[16,4,16,128]{3,2,1,0:T(8,128)} %get-tuple-element.54) | copy-start | bytes 1572868
  207.5 7.2 %collective-permute-start.8 = (f32[16,1,16,128]{3,2,1,0:T(8,128)S(1)}, f32[16,1,16,128]{3,2,1,0:T(8,128)S(1)}, u32[]{:S(2)}, u32[]{:S(2)}) collective-permute-start(f32[16,1,16,128]{3,2,1,0:T(8,128)S(1)} %get-tuple-element.75), channel_id=1, source_target_pairs={{1,0},{2,1},{3,2},{4,3},{5,4},{6,5},{7,6},{9,8},{10,9},{11,10},{12... | collective-permute-start | bytes 393224 | tf_op jit(solution)/shard_map/ppermute | solution.py:25
  208.9 7.1 %collective-permute-start.9 = (f32[16,1,16,128]{3,2,1,0:T(8,128)S(1)}, f32[16,1,16,128]{3,2,1,0:T(8,128)S(1)}, u32[]{:S(2)}, u32[]{:S(2)}) collective-permute-start(f32[16,1,16,128]{3,2,1,0:T(8,128)S(1)} %get-tuple-element.76), channel_id=1, source_target_pairs={{0,1},{1,2},{2,3},{3,4},{4,5},{5,6},{6,7},{8,9},{9,10},{10,11},{11... | collective-permute-start | bytes 393224 | tf_op jit(solution)/shard_map/ppermute | solution.py:22
  214.2 1.9 copy-start.18
  214.2 1.9 copy-start.21
  214.7 1.6 copy-start.7
  216.8 1.4 copy-start.8
  258.5 1.8 copy-start.4
  258.5 1.8 copy-start.44
  261.4 62.7 %copy-start.47 = (f32[64,256]{1,0:T(8,128)S(1)}, f32[64,256]{1,0:T(8,128)}, u32[]{:S(2)}) copy-start(f32[64,256]{1,0:T(8,128)} %param.17) | copy-start | bytes 196612
  261.5 62.7 %copy-start.48 = (f32[256]{0:T(256)S(1)}, f32[256]{0:T(256)}, u32[]{:S(2)}) copy-start(f32[256]{0:T(256)} %param.15) | copy-start | bytes 3076
  266.1 58.8 %copy-start.23 = (f32[16,2,4,16,128]{4,3,2,1,0:T(8,128)S(1)}, f32[16,2,4,16,128]{4,3,2,1,0:T(8,128)}, u32[]{:S(2)}) copy-start(f32[16,2,4,16,128]{4,3,2,1,0:T(8,128)} %copy-done.22) | copy-start | bytes 3145732
  329.6 1.3 copy-start.1
  (12 other events, 10.6 us)
Sparse Core Ops, SparseCore 0:
  49.6 31.8 all-gather.1
where the time goes:
time: 339 us; the launch traced here: 338 us
  blocking collectives  212 us (63%)
  other arithmetic  43.5 us (13%)
  starting transfers between devices  30.9 us (9%)
  local copies, waits for them, and re-layouts  25.9 us (8%)
  between operations  15.2 us (4%)
  matrix products  5.58 us (2%)
  waiting for transfers between devices  4.26 us (1%)
    psum x4, blocking collectives, local(): projected = lax.psum(local_dots, 'cell')  77 us
    psum x4, blocking collectives, local(): height = jnp.sqrt(lax.psum(inner(image, image), 'cell') + epsilon)  70.7 us
    psum x1, blocking collectives, local(): slab_pred = lax.psum(picked, 'cell')  35.7 us
    ppermute x5, starting transfers between devices, with_halo(): lax.ppermute(lax.slice_in_dim(block, block.shape[dim] - width, None, axis...  24.1 us
    psum x1, blocking collectives, local(): beta = jnp.sqrt(lax.psum(inner(rhs, rhs), 'cell') + epsilon)  23.5 us
    reduce_sum x9, other arithmetic, inner(): return jnp.sum(left * right, axis=(1, 2, 3, 4))  10.4 us
    ppermute x5, starting transfers between devices, with_halo(): lax.ppermute(lax.slice_in_dim(block, 0, width, axis=dim), axis, backward)  6.83 us
  transfers between devices with their start and end apart: 11, of which 3 were waited for; matrix products, arithmetic and copies ran while one was open for 18% of the time, Pallas kernels for 0%

commit v1 on v0

--- a/solution.py
+++ b/solution.py
@@ -110,6 +110,62 @@
     return solved
 
 
+SHIFTS = (2.0, 7.0, 4.5, 1.0)
+
+
+def krylov_coefficients(entries):
+    size = KRYLOV + 1
+    zero = jnp.zeros_like(entries[0])
+
+    def gram(row, col):
+        row, col = max(row, col), min(row, col)
+        return entries[row * (row + 1) // 2 + col]
+
+    def times_gram(coef):
+        out = []
+        for row in range(size):
+            total = zero
+            for col, value in enumerate(coef):
+                if value is not None:
+                    total = total + gram(row, col) * value
+            out.append(total)
+        return out
+
+    def dot(coef, image):
+        total = zero
+        for value, other in zip(coef, image):
+            if value is not None:
+                total = total + value * other
+        return total
+
+    beta = jnp.sqrt(gram(0, 0) + epsilon)
+    basis = [[1.0 / beta] + [None] * KRYLOV]
+    columns = []
+    for jdx in range(KRYLOV):
+        image = [None] * size
+        for idx in range(jdx + 1):
+            value = basis[jdx][idx]
+            base = SHIFTS[idx] * value
+            image[idx] = base if image[idx] is None else image[idx] + base
+            image[idx + 1] = value
+        mapped = times_gram(image)
+        projected = [dot(basis[idx], mapped) for idx in range(jdx + 1)]
+        for idx in range(jdx + 1):
+            for pos in range(idx + 1):
+                image[pos] = image[pos] - projected[idx] * basis[idx][pos]
+        height = jnp.sqrt(jnp.maximum(dot(image, times_gram(image)), 0.0) + epsilon)
+        columns.append(projected + [height])
+        basis.append([None if value is None else value / height for value in image])
+    solved = least_squares(columns, beta)
+    mixed = []
+    for pos in range(KRYLOV):
+        total = zero
+        for jdx in range(pos, KRYLOV):
+            total = total + solved[jdx] * basis[jdx][pos]
+        mixed.append(total)
+    return mixed
+
+
 def ensemble_weights(predicted, obs_values, obs_error, noise):
     members = predicted.shape[0]
     sigma = math.sqrt(inflation) * obs_error
@@ -158,22 +214,19 @@
     frac_x = frac_x * keep_face
     trans_y, frac_y, trans_z, frac_z = plane_faces(perm_pad[:, 1:-1], saturation)
     coeffs = (porosity / time_step, trans_x, frac_x, trans_y, frac_y, trans_z, frac_z)
-    columns = []
-    beta = jnp.sqrt(lax.psum(inner(rhs, rhs), "cell") + epsilon)
-    basis = [rhs / expand(beta)]
+    powers = [rhs]
     for jdx in range(KRYLOV):
-        vector = basis[jdx]
+        vector = powers[jdx]
         padded = with_halo(vector[:, 0], (("cell", 1),), 1)
         out_pressure, out_water = operator(padded, vector[:, 1], coeffs)
         image = jnp.stack([out_pressure, out_water], 1)
-        local_dots = jnp.stack([inner(basis[idx], image) for idx in range(jdx + 1)], 0)
-        projected = lax.psum(local_dots, "cell")
-        for idx in range(jdx + 1):
-            image = image - expand(projected[idx]) * basis[idx]
-        height = jnp.sqrt(lax.psum(inner(image, image), "cell") + epsilon)
-        columns.append([projected[idx] for idx in range(jdx + 1)] + [height])
-        basis.append(image / expand(height))
-    solved = least_squares(columns, beta)
+        powers.append(image - SHIFTS[jdx] * vector)
+    entries = jnp.stack(
+        [inner(powers[row], powers[col]) for row in range(KRYLOV + 1) for col in range(row + 1)], 0
+    )
+    entries = lax.psum(entries, "cell")
+    solved = krylov_coefficients(entries)
+    basis = powers
     increment = expand(solved[0]) * basis[0]
     for jdx in range(1, KRYLOV):
         increment = increment + expand(solved[jdx]) * basis[jdx]

time: 339 us -> 179 us (0.53)
  blocking collectives: 212 us -> 62.3 us
  other arithmetic: 43.5 us -> 31.3 us
  waiting for transfers between devices: 4.26 us -> 8.09 us
    psum x9 -> x1, blocking collectives: 171 us -> 22.9 us  [local(): entries = lax.psum(entries, 'cell')]
    reduce_sum x9 -> x1, other arithmetic: 10.4 us -> 1.75 us  [inner(): return jnp.sum(left * right, axis=(1, 2, 3, 4))]
    ppermute x5, waiting for transfers between devices: 4.21 us -> 7.86 us  [with_halo(): lax.ppermute(lax.slice_in_dim(block, block.shape[dim] - width, None, axis...]
  transfers between devices with their start and end apart: 11 -> 11, of which waited for: 3 -> 4; matrix products, arithmetic and copies ran while one was open for 18% -> 27% of each run, Pallas kernels for 0% -> 0%
where the time goes in v1:
time: 179 us
  blocking collectives  62.3 us (35%)
  starting transfers between devices  32.2 us (18%)
  other arithmetic  31.3 us (17%)
  local copies, waits for them, and re-layouts  24.3 us (14%)
  between operations  15 us (8%)
  waiting for transfers between devices  8.09 us (5%)
  matrix products  5.59 us (3%)
    psum x1, blocking collectives, local(): slab_pred = lax.psum(picked, 'cell')  34.2 us
    ppermute x5, starting transfers between devices, with_halo(): lax.ppermute(lax.slice_in_dim(block, block.shape[dim] - width, None, axis...  25.7 us
    psum x1, blocking collectives, local(): entries = lax.psum(entries, 'cell')  22.9 us
    ppermute x5, waiting for transfers between devices, with_halo(): lax.ppermute(lax.slice_in_dim(block, block.shape[dim] - width, None, axis...  7.86 us
    another operation x3, other arithmetic, ensemble_weights(): factor = jnp.linalg.cholesky(gram)  6.52 us
    ppermute x5, starting transfers between devices, with_halo(): lax.ppermute(lax.slice_in_dim(block, 0, width, axis=dim), axis, backward)  6.45 us
    another operation x2, other arithmetic, ensemble_weights(): return jax.scipy.linalg.cho_solve((factor, True), cross)  5.55 us
    all_gather x1, blocking collectives, local(): predicted = lax.all_gather(slab_pred, 'grp', axis=0, tiled=True)  5.24 us
  transfers between devices with their start and end apart: 11, of which 4 were waited for; matrix products, arithmetic and copies ran while one was open for 27% of the time, Pallas kernels for 0%

profile of v1, /device:TPU:0, one launch (start us, length us, event | category | flops | bytes accessed | tf_op | source)
XLA Modules:
  0.0 178.8 jit_solution(13443857201564413022)
XLA Ops:
  7.3 2.1 %fusion.63 = (f32[16,2,1,16,128]{4,3,2,0,1:T(8,128)}, f32[16,2,1,16,128]{4,3,2,0,1:T(8,128)}) fusion(f32[16,1,4,16,128]{4,3,2,0,1:T(8,128)} %bitcast.524, f32[16,1,4,16,128]{4,3,2,0,1:T(8,128)} %bitcast.553), kind=kLoop, calls=%fused_computation.168 | loop fusion | flops 131072 | bytes 1572864 | tf_op jit(solution)/shard_map/stack | solution.py:202
  9.4 4.9 %collective-permute-start = (f32[16,2,1,16,128]{4,3,2,0,1:T(8,128)}, f32[16,2,1,16,128]{4,3,2,0,1:T(8,128)S(1)}, u32[]{:S(2)}, u32[]{:S(2)}) collective-permute-start(f32[16,2,1,16,128]{4,3,2,0,1:T(8,128)} %get-tuple-element.92), channel_id=1, source_target_pairs={{0,1},{1,2},{2,3},{3,4},{4,5},{5,6},{6,7},{8,9},{9,10},{10,11},{11... | collective-permute-start | bytes 786440 | tf_op jit(solution)/shard_map/ppermute | solution.py:22
  14.2 1.3 collective-permute-start.1
  15.6 0.8 fusion.124
  16.4 1.3 collective-permute-start.2
  17.7 5.8 %collective-permute-start.3 = (f32[16,1,16,128]{3,2,1,0:T(8,128)}, f32[16,1,16,128]{3,2,1,0:T(8,128)}, u32[]{:S(2)}, u32[]{:S(2)}) collective-permute-start(f32[16,1,16,128]{3,2,1,0:T(8,128)} %get-tuple-element.107), channel_id=1, source_target_pairs={{0,1},{1,2},{2,3},{3,4},{4,5},{5,6},{6,7},{8,9},{9,10},{10,11},{11... | collective-permute-start | bytes 393224 | tf_op jit(solution)/shard_map/ppermute | solution.py:22
  23.7 1.0 copy-done.9
  24.8 1.6 bitcast_multiply_fusion
  26.5 1.9 %gather_fusion = s32[256]{0:T(256)S(1)} fusion(s32[128]{0:T(128)S(1)} %copy-done, s32[1024]{0:T(1024)S(1)} %pad_clamp_fusion.1), kind=kCustom, calls=%fused_computation | custom fusion | bytes 3072 | tf_op jit(solution)/shard_map/jit(_take)/gather | solution.py:236
  28.5 0.8 slice.609
  29.3 1.0 slice.615
  30.3 0.9 slice.491
  31.2 1.0 slice.499
  32.3 1.1 pad_maximum_fusion
  33.9 0.7 copy-done.8
  35.4 1.0 multiply_multiply_fusion.11
  36.4 0.6 fusion.113
  37.6 1.6 fusion.62
  39.1 0.5 fusion.52
  40.8 1.3 collective-permute-start.4
  42.1 4.8 %collective-permute-start.5 = (f32[16,1,16,128]{3,2,1,0:T(8,128)S(1)}, f32[16,1,16,128]{3,2,1,0:T(8,128)S(1)}, u32[]{:S(2)}, u32[]{:S(2)}) collective-permute-start(f32[16,1,16,128]{3,2,1,0:T(8,128)S(1)} %get-tuple-element.105), channel_id=1, source_target_pairs={{0,1},{1,2},{2,3},{3,4},{4,5},{5,6},{6,7},{8,9},{9,10},{10,11},{11... | collective-permute-start | bytes 393224 | tf_op jit(solution)/shard_map/ppermute | solution.py:22
  47.9 2.3 %collective-permute-done.5 = f32[16,1,16,128]{3,2,1,0:T(8,128)S(1)} collective-permute-done((f32[16,1,16,128]{3,2,1,0:T(8,128)S(1)}, f32[16,1,16,128]{3,2,1,0:T(8,128)S(1)}, u32[]{:S(2)}, u32[]{:S(2)}) %collective-permute-start.5) | collective-permute-done | bytes 131104 | tf_op jit(solution)/shard_map/ppermute | solution.py:22
  50.3 0.6 fusion.44
  50.9 0.5 fusion.40
  52.0 1.3 collective-permute-start.6
  53.3 5.2 %collective-permute-start.7 = (f32[16,1,16,128]{3,2,1,0:T(8,128)S(1)}, f32[16,1,16,128]{3,2,1,0:T(8,128)S(1)}, u32[]{:S(2)}, u32[]{:S(2)}) collective-permute-start(f32[16,1,16,128]{3,2,1,0:T(8,128)S(1)} %get-tuple-element.103), channel_id=1, source_target_pairs={{0,1},{1,2},{2,3},{3,4},{4,5},{5,6},{6,7},{8,9},{9,10},{10,11},{11... | collective-permute-start | bytes 393224 | tf_op jit(solution)/shard_map/ppermute | solution.py:22
  59.4 2.6 %collective-permute-done.7 = f32[16,1,16,128]{3,2,1,0:T(8,128)S(1)} collective-permute-done((f32[16,1,16,128]{3,2,1,0:T(8,128)S(1)}, f32[16,1,16,128]{3,2,1,0:T(8,128)S(1)}, u32[]{:S(2)}, u32[]{:S(2)}) %collective-permute-start.7) | collective-permute-done | bytes 131104 | tf_op jit(solution)/shard_map/ppermute | solution.py:22
  62.2 0.6 fusion.36
  62.8 0.5 fusion.32
  63.8 1.3 collective-permute-start.8
  65.1 5.0 %collective-permute-start.9 = (f32[16,1,16,128]{3,2,1,0:T(8,128)S(1)}, f32[16,1,16,128]{3,2,1,0:T(8,128)S(1)}, u32[]{:S(2)}, u32[]{:S(2)}) collective-permute-start(f32[16,1,16,128]{3,2,1,0:T(8,128)S(1)} %get-tuple-element.101), channel_id=1, source_target_pairs={{0,1},{1,2},{2,3},{3,4},{4,5},{5,6},{6,7},{8,9},{9,10},{10,11},{11... | collective-permute-start | bytes 393224 | tf_op jit(solution)/shard_map/ppermute | solution.py:22
  71.3 3.0 %collective-permute-done.9 = f32[16,1,16,128]{3,2,1,0:T(8,128)S(1)} collective-permute-done((f32[16,1,16,128]{3,2,1,0:T(8,128)S(1)}, f32[16,1,16,128]{3,2,1,0:T(8,128)S(1)}, u32[]{:S(2)}, u32[]{:S(2)}) %collective-permute-start.9) | collective-permute-done | bytes 131104 | tf_op jit(solution)/shard_map/ppermute | solution.py:22
  74.4 0.6 fusion.28
  75.5 0.7 copy-done.5
  76.2 1.7 multiply_reduce_fusion
  78.0 22.9 %psum.14 = f32[15,16]{1,0:T(8,128)S(1)} all-reduce(f32[15,16]{1,0:T(8,128)S(1)} %stack.139), channel_id=1, replica_groups=mesh['grp'=4,'cell'=8] {'cell'}, use_global_device_ids=true, to_apply=%region_15.16 | all-reduce | flops 240 | bytes 1920 | tf_op jit(solution)/shard_map/psum | solution.py:227
  101.1 2.0 %multiply_add_fusion = f32[16,2,4,16,128]{4,3,2,1,0:T(8,128)S(1)} fusion(f32[16,2,4,16,128]{4,3,2,1,0:T(8,128)} %copy-done.6, f32[16,2,4,16,128]{4,3,2,1,0:T(8,128)S(1)} %copy_subtract_fusion.2, f32[16,2,4,16,128]{4,3,2,1,0:T(8,128)S(1)} %copy_subtract_fusion.3, f32[16,2,4,16,128]{4,3,2,1,0:T(8,128)} %param.10, f32[16]{0:T(128)S(1)} %get-tuple-element.112, ...), kind=kLoop, calls=%fused_computation.18 | loop fusion | flops 1835008 | bytes 5243136 | tf_op jit(solution)/shard_map/add | solution.py:232
  103.4 0.8 copy-done.16
  104.2 4.6 %copy.62 = f32[16,2,4,16,128]{0,4,3,2,1:T(8,128)} copy(f32[16,2,4,16,128]{4,3,2,0,1:T(8,128)S(1)} %pad_maximum_fusion.6) | data formatting | bytes 2097152 | tf_op jit(solution)/shard_map/stack | solution.py:233
  108.9 4.2 %gather_fusion.1 = f32[256,16]{1,0:T(8,128)S(1)} fusion(f32[16,16384]{0,1:T(8,128)} %bitcast.536, s32[1024]{0:T(1024)S(1)} %pad_clamp_fusion), kind=kCustom, calls=%fused_computation.1 | custom fusion | bytes 33792 | tf_op jit(solution)/shard_map/jit(_take)/gather | solution.py:242
  113.2 34.2 %psum.15 = f32[16,256]{0,1:T(8,128)S(1)} all-reduce(f32[16,256]{0,1:T(8,128)S(1)} %multiply_bitcast_fusion), channel_id=1, replica_groups=mesh['grp'=4,'cell'=8] {'cell'}, use_global_device_ids=true, to_apply=%region_16.17 | all-reduce | flops 4096 | bytes 32768 | tf_op jit(solution)/shard_map/psum | solution.py:243
  147.5 5.2 %all_gather.6 = f32[64,256]{1,0:T(8,128)S(1)} all-gather(f32[16,256]{1,0:T(8,128)S(1)} %copy.63), channel_id=1, replica_groups=mesh['grp'=4,'cell'=8] {'grp'}, dimensions={0}, use_global_device_ids=true | all-gather | bytes 81920 | tf_op jit(solution)/shard_map/all_gather | solution.py:244
  153.1 5.8 %cholesky.17 = f32[64,64]{1,0:T(8,128)S(1)} custom-call(f32[64,64]{1,0:T(8,128)S(1)} %fusion.80), custom_call_target="Cholesky" | custom-call | tf_op jit(solution)/shard_map/jit(cholesky)/cholesky | solution.py:181
  159.0 0.6 compare_reduce_fusion
  159.6 0.7 fusion.74
  160.3 4.9 %custom-call.10 = f32[1,64,64]{1,2,0:T(8,128)S(1)} custom-call(f32[1,64,64]{2,1,0:T(8,128)S(1)} %fusion.74), custom_call_target="InvertDiagBlocksLowerTriangular" | custom-call | tf_op jit(solution)/shard_map/jit(_cho_solve)/triangular_solve | solution.py:182
  166.0 4.7 %fusion = f32[2,8,128,128]{3,1,2,0:T(8,128)S(1)} fusion(f32[64,16384]{1,0:T(8,128)} %all-gather.2.cloned.1.call-done, f32[2,8,128,128]{3,2,1,0:T(8,128)S(1)} %bitcast.535, f32[64,64]{0,1:T(8,128)S(1)} %fusion.75, s32[]{:T(128)S(6)} %select_n.96), kind=kOutput, calls=%fused_computation.4 | convolution fusion | flops 201588736 | bytes 6299652 | tf_op jit(solution)/shard_map/dot_general | solution.py:251
  170.9 1.1 slice_bitcast_fusion.1
  (130 shorter events, 10.3 us)
Async XLA Ops:
  7.2 19.3 %copy-start = (s32[128]{0:T(128)S(1)}, s32[128]{0:T(128)}, u32[]{:S(2)}) copy-start(s32[128]{0:T(128)} %param.18) | copy-start | bytes 1540
  7.2 8.4 %copy-start.4 = (f32[16,2,4,16,128]{4,3,2,1,0:T(8,128)S(1)}, f32[16,2,4,16,128]{4,3,2,1,0:T(8,128)}, u32[]{:S(2)}) copy-start(f32[16,2,4,16,128]{4,3,2,1,0:T(8,128)} %param.10) | copy-start | bytes 3145732
  7.2 158.8 %all-gather.2.cloned.1.call-start = ((), (), s32[]{:S(2)}) async-start(), calls=%async_computation | async-start | bytes 5242880 | tf_op jit(solution)/shard_map/all_gather | solution.py:253
  7.2 16.3 %copy-start.3 = (f32[16,4,16,128]{3,2,1,0:T(8,128)S(1)}, f32[16,4,16,128]{3,2,1,0:T(8,128)}, u32[]{:S(2)}) copy-start(f32[16,4,16,128]{3,2,1,0:T(8,128)} %param.12) | copy-start | bytes 1572868
  7.2 16.3 %copy-start.15 = (f32[16,4,16,128]{3,2,1,0:T(8,128)S(1)}, f32[16,4,16,128]{3,2,1,0:T(8,128)}, u32[]{:S(2)}) copy-start(f32[16,4,16,128]{3,2,1,0:T(8,128)} %param.11) | copy-start | bytes 1572868
  9.4 22.9 %collective-permute-start = (f32[16,2,1,16,128]{4,3,2,0,1:T(8,128)}, f32[16,2,1,16,128]{4,3,2,0,1:T(8,128)S(1)}, u32[]{:S(2)}, u32[]{:S(2)}) collective-permute-start(f32[16,2,1,16,128]{4,3,2,0,1:T(8,128)} %get-tuple-element.92), channel_id=1, source_target_pairs={{0,1},{1,2},{2,3},{3,4},{4,5},{5,6},{6,7},{8,9},{9,10},{10,11},{11... | collective-permute-start | bytes 786440 | tf_op jit(solution)/shard_map/ppermute | solution.py:22
  14.2 18.0 %collective-permute-start.1 = (f32[16,2,1,16,128]{4,3,2,0,1:T(8,128)}, f32[16,2,1,16,128]{4,3,2,0,1:T(8,128)}, u32[]{:S(2)}, u32[]{:S(2)}) collective-permute-start(f32[16,2,1,16,128]{4,3,2,0,1:T(8,128)} %get-tuple-element.93), channel_id=1, source_target_pairs={{1,0},{2,1},{3,2},{4,3},{5,4},{6,5},{7,6},{9,8},{10,9},{11,10},{12... | collective-permute-start | bytes 786440 | tf_op jit(solution)/shard_map/ppermute | solution.py:25
  15.6 14.7 %copy-start.7 = (f32[16,4,16,128]{3,2,1,0:T(8,128)}, f32[16,4,16,128]{3,2,1,0:T(8,128)S(1)}, u32[]{:S(2)}) copy-start(f32[16,4,16,128]{3,2,1,0:T(8,128)S(1)} %slice_bitcast_fusion.11) | copy-start | bytes 1572868
  16.4 21.2 %collective-permute-start.2 = (f32[16,1,16,128]{3,2,1,0:T(8,128)}, f32[16,1,16,128]{3,2,1,0:T(8,128)}, u32[]{:S(2)}, u32[]{:S(2)}) collective-permute-start(f32[16,1,16,128]{3,2,1,0:T(8,128)} %get-tuple-element.106), channel_id=1, source_target_pairs={{1,0},{2,1},{3,2},{4,3},{5,4},{6,5},{7,6},{9,8},{10,9},{11,10},{12... | collective-permute-start | bytes 393224 | tf_op jit(solution)/shard_map/ppermute | solution.py:25
  17.7 19.9 %collective-permute-start.3 = (f32[16,1,16,128]{3,2,1,0:T(8,128)}, f32[16,1,16,128]{3,2,1,0:T(8,128)}, u32[]{:S(2)}, u32[]{:S(2)}) collective-permute-start(f32[16,1,16,128]{3,2,1,0:T(8,128)} %get-tuple-element.107), channel_id=1, source_target_pairs={{0,1},{1,2},{2,3},{3,4},{4,5},{5,6},{6,7},{8,9},{9,10},{10,11},{11... | collective-permute-start | bytes 393224 | tf_op jit(solution)/shard_map/ppermute | solution.py:22
  23.7 1.1 copy-start.9
  24.8 1.7 copy-start.18
  26.5 3.8 %copy-start.2 = (f32[16,4,16,128]{3,2,1,0:T(8,128)S(1)}, f32[16,4,16,128]{3,2,1,0:T(8,128)}, u32[]{:S(2)}) copy-start(f32[16,4,16,128]{3,2,1,0:T(8,128)} %param.13) | copy-start | bytes 1572868
  29.3 2.9 %copy-start.19 = (f32[256]{0:T(256)S(1)}, f32[256]{0:T(256)}, u32[]{:S(2)}) copy-start(f32[256]{0:T(256)} %param.16) | copy-start | bytes 3076
  33.5 1.1 copy-start.8
  33.5 1.3 copy-start.11
  33.5 1.5 copy-start.12
  33.6 1.7 copy-start.13
  33.6 1.9 %copy-start.14 = (f32[16,4,16,127]{3,2,1,0:T(8,128)S(1)}, f32[16,4,16,127]{3,2,1,0:T(8,128)}, u32[]{:S(2)}) copy-start(f32[16,4,16,127]{3,2,1,0:T(8,128)} %slice.499) | copy-start | bytes 1560580
  40.8 7.1 %collective-permute-start.4 = (f32[16,1,16,128]{3,2,1,0:T(8,128)S(1)}, f32[16,1,16,128]{3,2,1,0:T(8,128)S(1)}, u32[]{:S(2)}, u32[]{:S(2)}) collective-permute-start(f32[16,1,16,128]{3,2,1,0:T(8,128)S(1)} %get-tuple-element.104), channel_id=1, source_target_pairs={{1,0},{2,1},{3,2},{4,3},{5,4},{6,5},{7,6},{9,8},{10,9},{11,10},{12... | collective-permute-start | bytes 393224 | tf_op jit(solution)/shard_map/ppermute | solution.py:25
  42.1 8.1 %collective-permute-start.5 = (f32[16,1,16,128]{3,2,1,0:T(8,128)S(1)}, f32[16,1,16,128]{3,2,1,0:T(8,128)S(1)}, u32[]{:S(2)}, u32[]{:S(2)}) collective-permute-start(f32[16,1,16,128]{3,2,1,0:T(8,128)S(1)} %get-tuple-element.105), channel_id=1, source_target_pairs={{0,1},{1,2},{2,3},{3,4},{4,5},{5,6},{6,7},{8,9},{9,10},{10,11},{11... | collective-permute-start | bytes 393224 | tf_op jit(solution)/shard_map/ppermute | solution.py:22
  52.0 7.5 %collective-permute-start.6 = (f32[16,1,16,128]{3,2,1,0:T(8,128)S(1)}, f32[16,1,16,128]{3,2,1,0:T(8,128)S(1)}, u32[]{:S(2)}, u32[]{:S(2)}) collective-permute-start(f32[16,1,16,128]{3,2,1,0:T(8,128)S(1)} %get-tuple-element.102), channel_id=1, source_target_pairs={{1,0},{2,1},{3,2},{4,3},{5,4},{6,5},{7,6},{9,8},{10,9},{11,10},{12... | collective-permute-start | bytes 393224 | tf_op jit(solution)/shard_map/ppermute | solution.py:25
  53.3 8.8 %collective-permute-start.7 = (f32[16,1,16,128]{3,2,1,0:T(8,128)S(1)}, f32[16,1,16,128]{3,2,1,0:T(8,128)S(1)}, u32[]{:S(2)}, u32[]{:S(2)}) collective-permute-start(f32[16,1,16,128]{3,2,1,0:T(8,128)S(1)} %get-tuple-element.103), channel_id=1, source_target_pairs={{0,1},{1,2},{2,3},{3,4},{4,5},{5,6},{6,7},{8,9},{9,10},{10,11},{11... | collective-permute-start | bytes 393224 | tf_op jit(solution)/shard_map/ppermute | solution.py:22
  63.5 12.0 %copy-start.6 = (f32[16,2,4,16,128]{4,3,2,1,0:T(8,128)}, f32[16,2,4,16,128]{4,3,2,1,0:T(8,128)S(1)}, u32[]{:S(2)}) copy-start(f32[16,2,4,16,128]{4,3,2,1,0:T(8,128)S(1)} %copy_subtract_fusion.1) | copy-start | bytes 3145732
  63.8 7.4 %collective-permute-start.8 = (f32[16,1,16,128]{3,2,1,0:T(8,128)S(1)}, f32[16,1,16,128]{3,2,1,0:T(8,128)S(1)}, u32[]{:S(2)}, u32[]{:S(2)}) collective-permute-start(f32[16,1,16,128]{3,2,1,0:T(8,128)S(1)} %get-tuple-element.100), channel_id=1, source_target_pairs={{1,0},{2,1},{3,2},{4,3},{5,4},{6,5},{7,6},{9,8},{10,9},{11,10},{12... | collective-permute-start | bytes 393224 | tf_op jit(solution)/shard_map/ppermute | solution.py:25
  65.1 9.1 %collective-permute-start.9 = (f32[16,1,16,128]{3,2,1,0:T(8,128)S(1)}, f32[16,1,16,128]{3,2,1,0:T(8,128)S(1)}, u32[]{:S(2)}, u32[]{:S(2)}) collective-permute-start(f32[16,1,16,128]{3,2,1,0:T(8,128)S(1)} %get-tuple-element.101), channel_id=1, source_target_pairs={{0,1},{1,2},{2,3},{3,4},{4,5},{5,6},{6,7},{8,9},{9,10},{10,11},{11... | collective-permute-start | bytes 393224 | tf_op jit(solution)/shard_map/ppermute | solution.py:22
  75.0 1.2 copy-start.5
  101.1 2.0 %copy-start.17 = (f32[16,4,16,128]{3,2,1,0:T(8,128)S(1)}, f32[16,4,16,128]{3,2,1,0:T(8,128)}, u32[]{:S(2)}) copy-start(f32[16,4,16,128]{3,2,1,0:T(8,128)} %param.14) | copy-start | bytes 1572868
  103.1 1.0 copy-start.16
  104.2 61.0 %copy-start.20 = (f32[64,256]{1,0:T(8,128)S(1)}, f32[64,256]{1,0:T(8,128)}, u32[]{:S(2)}) copy-start(f32[64,256]{1,0:T(8,128)} %param.17) | copy-start | bytes 196612
  104.2 61.0 %copy-start.21 = (f32[256]{0:T(256)S(1)}, f32[256]{0:T(256)}, u32[]{:S(2)}) copy-start(f32[256]{0:T(256)} %param.15) | copy-start | bytes 3076
  108.9 57.1 %copy-start.10 = (f32[16,2,4,16,128]{4,3,2,1,0:T(8,128)S(1)}, f32[16,2,4,16,128]{4,3,2,1,0:T(8,128)}, u32[]{:S(2)}) copy-start(f32[16,2,4,16,128]{4,3,2,1,0:T(8,128)} %copy-done.9) | copy-start | bytes 3145732
  170.7 1.3 copy-start.1
Sparse Core Ops, SparseCore 0:
  26.6 36.1 all-gather.1

commit v2 on v1

v2 whole, which is shorter than its diff:
```python
import functools
import math

import jax
import jax.numpy as jnp
from jax import lax
from jax.experimental import pallas as pl
from jax.experimental.pallas import tpu as pltpu
from jax.sharding import PartitionSpec as P

KRYLOV = 4
GROUPS = 4
SHIFTS = (1.5, 4.0, 8.0, 2.0)
MESH = pl.DeviceIdType.MESH

epsilon = 1e-06
time_step = 0.1
compress = 0.5
inflation = 4.0


def mobility(sat_field):
    return sat_field * sat_field + 0.5 * (1.0 - sat_field) * (1.0 - sat_field)


def face_pair(perm_low, perm_high, sat_low, sat_high):
    trans = (
        2.0
        * perm_low
        * perm_high
        / (perm_low + perm_high)
        * (0.5 * (mobility(sat_low) + mobility(sat_high)))
    )
    return (trans, trans * (0.5 * (sat_low + sat_high)))


def split3(value):
    high = value.astype(jnp.bfloat16)
    rest = value - high.astype(jnp.float32)
    middle = rest.astype(jnp.bfloat16)
    low = (rest - middle.astype(jnp.float32)).astype(jnp.bfloat16)
    return high, middle, low


def least_squares(columns, beta):
    rows = [list(column) for column in columns]
    cosines = []
    sines = []
    target = [beta] + [jnp.zeros_like(beta) for column in columns]
    for jdx in range(len(rows)):
        column = rows[jdx]
        for idx in range(jdx):
            upper = cosines[idx] * column[idx] + sines[idx] * column[idx + 1]
            column[idx + 1] = -sines[idx] * column[idx] + cosines[idx] * column[idx + 1]
            column[idx] = upper
        radius = jnp.sqrt(column[jdx] * column[jdx] + column[jdx + 1] * column[jdx + 1])
        cosines.append(column[jdx] / radius)
        sines.append(column[jdx + 1] / radius)
        column[jdx] = radius
        target[jdx + 1] = -sines[jdx] * target[jdx]
        target[jdx] = cosines[jdx] * target[jdx]
    count = len(rows)
    solved = [None] * count
    for jdx in reversed(range(count)):
        partial_sum = target[jdx]
        for idx in range(jdx + 1, count):
            partial_sum = partial_sum - rows[idx][jdx] * solved[idx]
        solved[jdx] = partial_sum / rows[jdx][jdx]
    return solved

def krylov_coefficients(entries):
    size = KRYLOV + 1
    zero = jnp.zeros_like(entries[0])

    def gram(row, col):
        row, col = max(row, col), min(row, col)
        return entries[row * (row + 1) // 2 + col]

    def times_gram(coef):
        out = []
        for row in range(size):
            total = zero
            for col, value in enumerate(coef):
                if value is not None:
                    total = total + gram(row, col) * value
            out.append(total)
        return out

    def dot(coef, image):
        total = zero
        for value, other in zip(coef, image):
            if value is not None:
                total = total + value * other
        return total

    beta = jnp.sqrt(gram(0, 0) + epsilon)
    basis = [[1.0 / beta] + [None] * KRYLOV]
    columns = []
    for jdx in range(KRYLOV):
        image = [None] * size
        for idx in range(jdx + 1):
            value = basis[jdx][idx]
            base = SHIFTS[idx] * value
            image[idx] = base if image[idx] is None else image[idx] + base
            image[idx + 1] = value
        mapped = times_gram(image)
        projected = [dot(basis[idx], mapped) for idx in range(jdx + 1)]
        for idx in range(jdx + 1):
            for pos in range(idx + 1):
                image[pos] = image[pos] - projected[idx] * basis[idx][pos]
        height = jnp.sqrt(jnp.maximum(dot(image, times_gram(image)), 0.0) + epsilon)
        columns.append(projected + [height])
        basis.append([None if value is None else value / height for value in image])
    solved = least_squares(columns, beta)
    mixed = []
    for pos in range(KRYLOV):
        total = zero
        for jdx in range(pos, KRYLOV):
            total = total + solved[jdx] * basis[jdx][pos]
        mixed.append(total)
    return mixed


def solve_kernel(
    cell_count, grp_count,
    rhs, lperm, poro, sat, pres, cells,
    inc_out, pred_out,
    powers, tx, gx, ty, gy, tz, gz, halo, gram, gslots, coefs, lhs, pslots, wslots,
    halo_send, halo_recv, gram_send, gram_recv, pick_send, pick_recv, pred_send, pred_recv,
):
    me = lax.axis_index("cell")
    mine = lax.axis_index("grp")
    members, _, slab, rows, cols = rhs.shape
    group = members // GROUPS
    has_prev, has_next = me > 0, me < cell_count - 1

    barrier = pltpu.get_barrier_semaphore()
    for step in range(1, cell_count):
        pl.semaphore_signal(
            barrier, inc=1, device_id={"cell": lax.rem(me + step, cell_count)}, device_id_type=MESH
        )
    for step in range(1, grp_count):
        pl.semaphore_signal(
            barrier, inc=1, device_id={"grp": lax.rem(mine + step, grp_count)}, device_id_type=MESH
        )
    pl.semaphore_wait(barrier, cell_count + grp_count - 2)

    def plane(field, part, at):
        part = pl.ds(part * group, group)
        if field == 0:
            return lperm.at[part, at]
        if field == 1:
            return sat.at[part, at]
        if field == 2:
            return rhs.at[part, 0, at]
        return powers.at[field - 3, part, 0, at]

    def halo_copy(field, part, side):
        return pltpu.make_async_remote_copy(
            src_ref=plane(field, part, slab - 1 if side == 0 else 0),
            dst_ref=halo.at[side, field, pl.ds(part * group, group)],
            send_sem=halo_send.at[side, field, part],
            recv_sem=halo_recv.at[side, field, part],
            device_id={"cell": (me + 1 if side == 0 else me + cell_count - 1) % cell_count},
            device_id_type=MESH,
        )

    def start_halo(field, part):
        @pl.when(has_next)
        def _():
            halo_copy(field, part, 0).start()

        @pl.when(has_prev)
        def _():
            halo_copy(field, part, 1).start()

    def wait_halo(field, part):
        @pl.when(has_prev)
        def _():
            halo_copy(field, part, 0).wait_recv()

        @pl.when(has_next)
        def _():
            halo_copy(field, part, 1).wait_recv()

    for part in range(GROUPS):
        for field in range(3):
            start_halo(field, part)

    @pl.when(me == 0)
    def _():
        halo[0] = jnp.zeros(halo.shape[1:], jnp.float32)

    @pl.when(me == cell_count - 1)
    def _():
        halo[1] = jnp.zeros(halo.shape[1:], jnp.float32)

    row_at = lax.broadcasted_iota(jnp.int32, (rows, cols), 0)
    col_at = lax.broadcasted_iota(jnp.int32, (rows, cols), 1)
    keep_rows = (row_at < rows - 1).astype(jnp.float32)
    keep_cols = (col_at < cols - 1).astype(jnp.float32)
    keep_low = has_prev.astype(jnp.float32)
    keep_high = has_next.astype(jnp.float32)

    def down(value, axis):
        return pltpu.roll(value, value.shape[axis] - 1, axis)

    def up(value, axis):
        return pltpu.roll(value, 1, axis)

    def inner_coeffs(m, carry):
        perm = [jnp.exp(lperm[m, x]) for x in range(slab)]
        water = [sat[m, x] for x in range(slab)]
        for x in range(slab):
            trans, frac = face_pair(perm[x], down(perm[x], 0), water[x], down(water[x], 0))
            ty[m, x] = trans * keep_rows
            gy[m, x] = frac * keep_rows
            trans, frac = face_pair(perm[x], down(perm[x], 1), water[x], down(water[x], 1))
            tz[m, x] = trans * keep_cols
            gz[m, x] = frac * keep_cols
            if x:
                trans, frac = face_pair(perm[x - 1], perm[x], water[x - 1], water[x])
                tx[m, x] = trans
                gx[m, x] = frac
        return carry

    lax.fori_loop(0, members, inner_coeffs, 0)

    def edge_coeffs(m):
        trans, frac = face_pair(jnp.exp(halo[0, 0, m]), jnp.exp(lperm[m, 0]), halo[0, 1, m], sat[m, 0])
        tx[m, 0] = trans * keep_low
        gx[m, 0] = frac * keep_low
        trans, frac = face_pair(
            jnp.exp(lperm[m, slab - 1]), jnp.exp(halo[1, 0, m]), sat[m, slab - 1], halo[1, 1, m]
        )
        tx[m, slab] = trans * keep_high
        gx[m, slab] = frac * keep_high

    def load(step, m, which, x):
        return rhs[m, which, x] if step == 0 else powers[step - 1, m, which, x]

    def apply(step, m):
        first = [halo[0, 2 + step, m]] + [load(step, m, 0, x) for x in range(slab)] + [halo[1, 2 + step, m]]
        flow_t, flow_g = [], []
        for x in range(slab + 1):
            diff = first[x + 1] - first[x]
            flow_t.append(tx[m, x] * diff)
            flow_g.append(gx[m, x] * diff)
        sums = [None] * (step + 2)
        start = None
        for x in range(slab):
            here = first[x + 1]
            second = load(step, m, 1, x)
            diff_y = down(here, 0) - here
            diff_z = down(here, 1) - here

            def net(flow_x, coef_y, coef_z):
                flow_y = coef_y * diff_y
                flow_z = coef_z * diff_z
                return (
                    flow_x[x] - flow_x[x + 1] + (up(flow_y, 0) - flow_y) + (up(flow_z, 1) - flow_z)
                )

            accum = poro[m, x] * (1.0 / time_step)
            out_u = accum * (compress * here + 0.5 * second) + net(flow_t, ty[m, x], tz[m, x])
            out_w = accum * second + net(flow_g, gy[m, x], gz[m, x])
            out_u = out_u - SHIFTS[step] * here
            out_w = out_w - SHIFTS[step] * second
            if step < KRYLOV - 1:
                powers[step, m, 0, x] = out_u
                powers[step, m, 1, x] = out_w
            for other in range(step + 2):
                if other == step + 1:
                    term = out_u * out_u + out_w * out_w
                elif other == step:
                    term = here * out_u + second * out_w
                else:
                    term = load(other, m, 0, x) * out_u + load(other, m, 1, x) * out_w
                sums[other] = term if x == 0 else sums[other] + term
            if step == 0:
                term = here * here + second * second
                start = term if x == 0 else start + term
        row = step + 1
        for other in range(step + 2):
            gram[row * (row + 1) // 2 + other, pl.ds(m, 1), :] = jnp.sum(
                sums[other], axis=0, keepdims=True
            )
        if step == 0:
            gram[0, pl.ds(m, 1), :] = jnp.sum(start, axis=0, keepdims=True)

    for step in range(KRYLOV):
        for part in range(GROUPS):
            if step == 0:
                wait_halo(0, part)
                wait_halo(1, part)
            wait_halo(2 + step, part)

            def body(m, carry):
                if step == 0:
                    edge_coeffs(m)
                apply(step, m)
                return carry

            lax.fori_loop(part * group, (part + 1) * group, body, 0)
            if step < KRYLOV - 1:
                start_halo(3 + step, part)

    def exchange(slots, here, count, axis, send, recv):
        copies = []
        for step in range(1, count):
            copies.append(
                pltpu.make_async_remote_copy(
                    src_ref=slots.at[here],
                    dst_ref=slots.at[here],
                    send_sem=send.at[step],
                    recv_sem=recv.at[step],
                    device_id={axis: lax.rem(here + step, count)},
                    device_id_type=MESH,
                )
            )
        for copy in copies:
            copy.start()
        for step in range(1, count):
            source = lax.rem(here + count - step, count)
            pltpu.make_async_remote_copy(
                src_ref=slots.at[source],
                dst_ref=slots.at[source],
                send_sem=send.at[step],
                recv_sem=recv.at[step],
                device_id={axis: lax.rem(here + step, count)},
                device_id_type=MESH,
            ).wait_recv()
        return copies

    pending = []
    count = (KRYLOV + 1) * (KRYLOV + 2) // 2
    lane = lax.broadcasted_iota(jnp.int32, (members, cols), 1)
    tile = jnp.zeros((members, cols), jnp.float32)
    for entry in range(count):
        tile = jnp.where(lane == entry, jnp.sum(gram[entry], axis=1, keepdims=True), tile)
    gslots[me] = tile
    pending += exchange(gslots, me, cell_count, "cell", gram_send, gram_recv)
    total = gslots[0]
    for slot in range(1, cell_count):
        total = total + gslots[slot]
    mixed = krylov_coefficients([total[:, entry : entry + 1] for entry in range(count)])
    for idx in range(KRYLOV):
        coefs[idx] = jnp.broadcast_to(mixed[idx], (members, cols))

    def combine(m, carry):
        scale = [coefs[idx, pl.ds(m, 1), :] for idx in range(KRYLOV)]
        for which in range(2):
            for x in range(slab):
                total = scale[0] * rhs[m, which, x]
                for idx in range(1, KRYLOV):
                    total = total + scale[idx] * powers[idx - 1, m, which, x]
                inc_out[m, which, x] = total
                state = (pres if which == 0 else sat)[m, x] + total
                at = pl.ds(pl.multiple_of(m * (slab * rows) + x * rows, rows), rows)
                for idx, piece in enumerate(split3(state)):
                    lhs[which, at, idx * cols : (idx + 1) * cols] = piece
        return carry

    lax.fori_loop(0, members, combine, 0)
    wells = cells.shape[1] // 2
    for which in range(2):
        cell = cells[:, which * wells : (which + 1) * wells]
        pick_col = lax.broadcasted_iota(jnp.int32, (cols, wells), 0) == lax.rem(cell, cols)
        pick_col = pick_col.astype(jnp.float32).astype(jnp.bfloat16)
        pick_row = (
            lax.broadcasted_iota(jnp.int32, (slab * rows, wells), 0) + me * (slab * rows)
            == lax.div(cell, cols)
        ).astype(jnp.float32)
        found = jnp.dot(
            lhs[which],
            jnp.concatenate([pick_col, pick_col, pick_col], axis=0),
            preferred_element_type=jnp.float32,
        )
        found = found.reshape(members, slab * rows, wells) * pick_row[None]
        pslots[me, :, which * wells : (which + 1) * wells] = jnp.sum(found, axis=1)
    pending += exchange(pslots, me, cell_count, "cell", pick_send, pick_recv)
    total = pslots[0]
    for slot in range(1, cell_count):
        total = total + pslots[slot]
    wslots[mine] = total
    pending += exchange(wslots, mine, grp_count, "grp", pred_send, pred_recv)
    pred_out[...] = wslots[...]
    for copy in pending:
        copy.wait_send()
    for field in range(2 + KRYLOV):
        for part in range(GROUPS):

            @pl.when(has_next)
            def _():
                halo_copy(field, part, 0).wait_send()

            @pl.when(has_prev)
            def _():
                halo_copy(field, part, 1).wait_send()


def dot3(left, right, dims):
    dot = functools.partial(
        lax.dot_general, dimension_numbers=(dims, ((), ())), preferred_element_type=jnp.float32
    )
    a = split3(left)
    b = split3(right)
    small = dot(a[0], b[2]) + dot(a[2], b[0]) + dot(a[1], b[1])
    return dot(a[0], b[0]) + (small + (dot(a[0], b[1]) + dot(a[1], b[0])))


def update_kernel(
    pred, obs, err, noise, all_perm, all_poro, own_perm, own_poro, perm_out, poro_out
):
    members = pred.shape[0]
    local_members = own_perm.shape[0]
    offset = lax.axis_index("grp") * local_members
    rows, cols = own_perm.shape[1:]
    sigma = math.sqrt(inflation) * err[...]
    predicted = pred[...]
    center = jnp.sum(predicted, axis=0, keepdims=True) * (1.0 / members)
    spread = (predicted - center) / (math.sqrt(members - 1.0) * sigma)
    innov = (obs[...] + sigma * noise[...] - predicted) / sigma
    row_at = lax.broadcasted_iota(jnp.int32, (members, members), 0)
    col_at = lax.broadcasted_iota(jnp.int32, (members, members), 1)
    gram = dot3(spread, spread, ((1,), (1,))) + (row_at == col_at).astype(jnp.float32)
    cross = dot3(spread, innov, ((1,), (1,)))
    both = jnp.concatenate([gram, cross], axis=1)
    line = lax.broadcasted_iota(jnp.int32, (members, 2 * members), 0)
    for k in range(members):
        pivot = both[k : k + 1, :] / both[k : k + 1, k : k + 1]
        factor = both[:, k : k + 1]
        both = jnp.where(line == k, pivot, both - factor * pivot)
    weights = both[:, members:]
    pick = (
        lax.broadcasted_iota(jnp.int32, (local_members, members), 0) + offset
        == lax.broadcasted_iota(jnp.int32, (local_members, members), 1)
    ).astype(jnp.float32)
    own = dot3(pick, weights, ((1,), (1,))) * (1.0 / math.sqrt(members - 1.0))
    high, middle, _ = split3(own)
    left = jnp.concatenate([high, middle, high], axis=1)
    for source, base, out in ((all_perm, own_perm, perm_out), (all_poro, own_poro, poro_out)):
        for row in range(0, rows, 2):
            block = jnp.concatenate([source[:, row, :], source[:, row + 1, :]], axis=1)
            top = block.astype(jnp.bfloat16)
            rest = (block - top.astype(jnp.float32)).astype(jnp.bfloat16)
            right = jnp.concatenate([top, top, rest], axis=0)
            update = jnp.dot(left, right, preferred_element_type=jnp.float32)
            out[:, row, :] = base[:, row, :] + update[:, :cols]
            out[:, row + 1, :] = base[:, row + 1, :] + update[:, cols:]


def local(
    rhs, log_perm, porosity, saturation, pressure, obs_values, obs_error, noise, well_cell, obs_well
):
    members, slab, rows, cols = log_perm.shape
    all_members, observations = noise.shape
    cell_count = lax.axis_size("cell")
    grp_count = lax.axis_size("grp")
    wells = well_cell.shape[0]
    hit = obs_well[:, None] == jnp.arange(wells, dtype=jnp.int32)[None, :]
    cells = jnp.sum(jnp.where(hit, well_cell[None, :], 0), axis=1, dtype=jnp.int32)[None, :]
    all_perm = lax.all_gather(log_perm, "grp", axis=0, tiled=True)
    all_poro = lax.all_gather(porosity, "grp", axis=0, tiled=True)
    vmem = pl.BlockSpec(memory_space=pltpu.VMEM)
    f32 = jnp.float32
    field = (members, slab, rows, cols)
    face = (members, slab + 1, rows, cols)
    entries = (KRYLOV + 1) * (KRYLOV + 2) // 2
    increment, predicted = pl.pallas_call(
        functools.partial(solve_kernel, cell_count, grp_count),
        out_shape=(
            jax.ShapeDtypeStruct(rhs.shape, f32),
            jax.ShapeDtypeStruct((grp_count, members, observations), f32),
        ),
        in_specs=[vmem] * 6,
        out_specs=(vmem, vmem),
        scratch_shapes=[
            pltpu.VMEM((KRYLOV - 1,) + rhs.shape, f32),
            pltpu.VMEM(face, f32),
            pltpu.VMEM(face, f32),
            pltpu.VMEM(field, f32),
            pltpu.VMEM(field, f32),
            pltpu.VMEM(field, f32),
            pltpu.VMEM(field, f32),
            pltpu.VMEM((2, 2 + KRYLOV, members, rows, cols), f32),
            pltpu.VMEM((entries, members, cols), f32),
            pltpu.VMEM((cell_count, members, cols), f32),
            pltpu.VMEM((KRYLOV, members, cols), f32),
            pltpu.VMEM((2, members * slab * rows, 3 * cols), jnp.bfloat16),
            pltpu.VMEM((cell_count, members, observations), f32),
            pltpu.VMEM((grp_count, members, observations), f32),
            pltpu.SemaphoreType.DMA((2, 2 + KRYLOV, GROUPS)),
            pltpu.SemaphoreType.DMA((2, 2 + KRYLOV, GROUPS)),
            pltpu.SemaphoreType.DMA((cell_count,)),
            pltpu.SemaphoreType.DMA((cell_count,)),
            pltpu.SemaphoreType.DMA((cell_count,)),
            pltpu.SemaphoreType.DMA((cell_count,)),
            pltpu.SemaphoreType.DMA((grp_count,)),
            pltpu.SemaphoreType.DMA((grp_count,)),
        ],
        compiler_params=pltpu.CompilerParams(
            collective_id=0, has_side_effects=True, vmem_limit_bytes=40 * 2**20
        ),
        cost_estimate=pl.CostEstimate(flops=10**8, bytes_accessed=10**8, transcendentals=0),
    )(rhs, log_perm, porosity, saturation, pressure, cells)
    flat = (members, slab * rows, cols)
    wide = (all_members, slab * rows, cols)
    perm_post, poro_post = pl.pallas_call(
        update_kernel,
        out_shape=(jax.ShapeDtypeStruct(flat, f32), jax.ShapeDtypeStruct(flat, f32)),
        in_specs=[vmem] * 8,
        out_specs=(vmem, vmem),
        compiler_params=pltpu.CompilerParams(vmem_limit_bytes=40 * 2**20),
    )(
        predicted.reshape(all_members, observations),
        obs_values[None, :],
        obs_error[None, :],
        noise,
        all_perm.reshape(wide),
        all_poro.reshape(wide),
        log_perm.reshape(flat),
        porosity.reshape(flat),
    )
    return (increment, perm_post.reshape(field), poro_post.reshape(field))


def solution(mesh):
    in_specs = (
        P("grp", None, "cell", None, None),
        P("grp", "cell", None, None),
        P("grp", "cell", None, None),
        P("grp", "cell", None, None),
        P("grp", "cell", None, None),
        P(),
        P(),
        P(),
        P(),
        P(),
    )
    out_specs = (
        P("grp", None, "cell", None, None),
        P("grp", "cell", None, None),
        P("grp", "cell", None, None),
    )
    return jax.shard_map(local, mesh=mesh, in_specs=in_specs, out_specs=out_specs, check_vma=False)
```

time: 179 us -> 95.3 us (0.53)
  Pallas kernels: 0 us -> 68.8 us
  blocking collectives: 62.3 us -> 0 us
  starting transfers between devices: 32.2 us -> 0.08 us
  other arithmetic: 31.3 us -> 0.87 us
  local copies, waits for them, and re-layouts: 24.3 us -> 9.56 us
  waiting for transfers between devices: 8.09 us -> 1.42 us
  matrix products: 5.59 us -> 0 us
    pallas_call x0 -> x2, Pallas kernels: none -> 68.8 us  [the longest x1 58.3 us: local(): pl.pallas_call(functools.partial(solve_kernel, cell_count, grp_count), ou...]
    psum x2 -> x0, blocking collectives: 57.1 us -> none  [the longest x1 34.2 us: local(): slab_pred = lax.psum(picked, 'cell')]
    ppermute x10 -> x0, starting transfers between devices: 32.2 us -> none  [the longest x5 25.7 us: with_halo(): lax.ppermute(lax.slice_in_dim(block, block.shape[dim] - width, None, axis...]
    another operation x17 -> x0, other arithmetic: 18.7 us -> none  [the longest x3 6.52 us: ensemble_weights(): factor = jnp.linalg.cholesky(gram)]
    ppermute x10 -> x0, waiting for transfers between devices: 8.05 us -> none  [the longest x5 7.86 us: with_halo(): lax.ppermute(lax.slice_in_dim(block, block.shape[dim] - width, None, axis...]
    slice x39 -> x0, local copies, waits for them, and re-layouts: 7.53 us -> none  [the longest x8 1.6 us: net(): jnp.roll(flow_z, 1, -1) - flow_z]
    mul x12 -> x0, other arithmetic: 6.83 us -> none  [the longest x5 3.05 us: net(): flow_z = coef_z * diff_z]
    gather x2 -> x0, local copies, waits for them, and re-layouts: 6.06 us -> none  [the longest x1 4.19 us: local(): jnp.take(flat, component * cells_dev + local_cell, axis=1)]
  transfers between devices with their start and end apart: 11 -> 2, of which waited for: 4 -> 0; matrix products, arithmetic and copies ran while one was open for 27% -> 1% of each run, Pallas kernels for 0% -> 61%
where the time goes in v2:
time: 95.3 us; the launch traced here: 94.9 us
  Pallas kernels  68.8 us (72%)
  between operations  14.2 us (15%)
  local copies, waits for them, and re-layouts  9.56 us (10%)
  waiting for transfers between devices  1.42 us (1%)
    pallas_call x1, Pallas kernels, local(): pl.pallas_call(functools.partial(solve_kernel, cell_count, grp_count), ou...  58.3 us
    pallas_call x1, Pallas kernels, local(): pl.pallas_call(update_kernel, out_shape=(jax.ShapeDtypeStruct(flat, f32),...  10.4 us
    unnamed x25, local copies, waits for them, and re-layouts  9.56 us
  transfers between devices with their start and end apart: 2, of which 0 were waited for; matrix products, arithmetic and copies ran while one was open for 1% of the time, Pallas kernels for 61%

profile of v2, /device:TPU:0, one launch (start us, length us, event | category | flops | bytes accessed | tf_op | source)
XLA Modules:
  0.0 94.9 jit_solution(6306906250421588490)
XLA Ops:
  7.2 0.0 copy-start.1
  7.2 0.0 copy-start.3
  7.2 0.0 copy-start.11
  7.2 0.0 copy-start.10
  7.2 0.0 all-gather.3.cloned.1.call-start
  7.3 0.7 all-gather.3.cloned.1.call-update
  7.9 0.0 all-gather.5.cloned.1.call-start
  8.0 0.7 all-gather.5.cloned.1.call-update
  8.7 0.9 select_reduce_fusion
  9.6 0.0 copy-start
  9.6 1.0 %copy-done = f32[16,4,16,128]{3,2,1,0:T(8,128)S(1)} copy-done((f32[16,4,16,128]{3,2,1,0:T(8,128)S(1)}, f32[16,4,16,128]{3,2,1,0:T(8,128)}, u32[]{:S(2)}) %copy-start) | copy-done | bytes 524312
  10.6 0.0 copy-start.2
  10.6 1.0 %copy-done.2 = f32[16,4,16,128]{3,2,1,0:T(8,128)S(1)} copy-done((f32[16,4,16,128]{3,2,1,0:T(8,128)S(1)}, f32[16,4,16,128]{3,2,1,0:T(8,128)}, u32[]{:S(2)}) %copy-start.2) | copy-done | bytes 524312
  11.7 0.0 copy-start.6
  11.7 1.2 %copy-done.6 = f32[16,2,4,16,128]{4,3,2,1,0:T(8,128)S(1)} copy-done((f32[16,2,4,16,128]{4,3,2,1,0:T(8,128)S(1)}, f32[16,2,4,16,128]{4,3,2,1,0:T(8,128)}, u32[]{:S(2)}) %copy-start.6) | copy-done | bytes 1048600
  12.9 0.0 copy-start.7
  12.9 1.0 %copy-done.7 = f32[16,4,16,128]{3,2,1,0:T(8,128)S(1)} copy-done((f32[16,4,16,128]{3,2,1,0:T(8,128)S(1)}, f32[16,4,16,128]{3,2,1,0:T(8,128)}, u32[]{:S(2)}) %copy-start.7) | copy-done | bytes 524312
  13.9 0.0 copy-start.8
  13.9 1.0 %copy-done.8 = f32[16,4,16,128]{3,2,1,0:T(8,128)S(1)} copy-done((f32[16,4,16,128]{3,2,1,0:T(8,128)S(1)}, f32[16,4,16,128]{3,2,1,0:T(8,128)}, u32[]{:S(2)}) %copy-start.8) | copy-done | bytes 524312
  15.0 0.0 copy-start.9
  15.0 58.3 %shard_map.121 = (f32[16,2,4,16,128]{4,3,2,1,0:T(8,128)S(1)}, f32[4,16,256]{2,1,0:T(8,128)S(1)}) custom-call(f32[16,2,4,16,128]{4,3,2,1,0:T(8,128)S(1)} %copy-done.6, f32[16,4,16,128]{3,2,1,0:T(8,128)S(1)} %copy-done, f32[16,4,16,128]{3,2,1,0:T(8,128)S(1)} %copy-done.2, f32[16,4,16,128]{3,2,1,0:T(8,128)S(1)} %copy-done.7, f32[16,4,16,128]{3,2,1,0:T(8,128)S(1)} %copy-done.8, ...), custom_call_target="tpu_custom_call" | custom-call | flops 100000000 | bytes 100000000 | tf_op jit(solution)/shard_map/pallas_call | solution.py:470
  73.3 0.0 all-gather.3.cloned.1.call-done
  73.4 0.0 all-gather.5.cloned.1.call-done
  73.4 0.0 copy-done.1
  73.4 0.0 copy-done.3
  73.4 0.0 copy-done.11
  73.4 0.0 copy-done.10
  73.4 0.0 copy-done.9
  73.4 0.0 copy-start.4
  73.4 1.6 %copy-done.4 = f32[64,4,16,128]{3,2,1,0:T(8,128)S(1)} copy-done((f32[64,4,16,128]{3,2,1,0:T(8,128)S(1)}, f32[64,4,16,128]{3,2,1,0:T(8,128)}, u32[]{:S(2)}) %copy-start.4) | copy-done | bytes 2097176
  75.0 0.0 copy-start.5
  75.0 1.6 %copy-done.5 = f32[64,4,16,128]{3,2,1,0:T(8,128)S(1)} copy-done((f32[64,4,16,128]{3,2,1,0:T(8,128)S(1)}, f32[64,4,16,128]{3,2,1,0:T(8,128)}, u32[]{:S(2)}) %copy-start.5) | copy-done | bytes 2097176
  76.6 10.4 %shard_map.122 = (f32[16,64,128]{2,1,0:T(8,128)}, f32[16,64,128]{2,1,0:T(8,128)}) custom-call(f32[64,256]{1,0:T(8,128)S(1)} %bitcast.14, f32[1,256]{1,0:T(1,128)S(1)} %bitcast.16, f32[1,256]{1,0:T(1,128)S(1)} %bitcast.17, f32[64,256]{1,0:T(8,128)S(1)} %copy-done.9, f32[64,64,128]{2,1,0:T(8,128)S(1)} %bitcast.12, f32[64,64,128]{2,1,0:T(8,128)S(1)} %bitcast.13, ...), custom_call_target="tpu_custom_call" | custom-call | tf_op jit(solution)/shard_map/pallas_call | solution.py:509
  87.1 1.0 %copy.14 = f32[16,2,4,16,128]{4,3,2,1,0:T(8,128)} copy(f32[16,2,4,16,128]{4,3,2,1,0:T(8,128)S(1)} %get-tuple-element.14) | data formatting | bytes 2097152
Async XLA Ops:
  7.2 66.2 %copy-start.1 = (f32[16,4,16,128]{3,2,1,0:T(8,128)S(1)}, f32[16,4,16,128]{3,2,1,0:T(8,128)}, u32[]{:S(2)}) copy-start(f32[16,4,16,128]{3,2,1,0:T(8,128)} %lperm.1) | copy-start | bytes 1572868
  7.2 66.2 %copy-start.3 = (f32[16,4,16,128]{3,2,1,0:T(8,128)S(1)}, f32[16,4,16,128]{3,2,1,0:T(8,128)}, u32[]{:S(2)}) copy-start(f32[16,4,16,128]{3,2,1,0:T(8,128)} %poro.1) | copy-start | bytes 1572868
  7.2 66.2 %copy-start.11 = (f32[256]{0:T(256)S(1)}, f32[256]{0:T(256)}, u32[]{:S(2)}) copy-start(f32[256]{0:T(256)} %param.16) | copy-start | bytes 3076
  7.2 66.2 %copy-start.10 = (f32[256]{0:T(256)S(1)}, f32[256]{0:T(256)}, u32[]{:S(2)}) copy-start(f32[256]{0:T(256)} %param.15) | copy-start | bytes 3076
  7.2 66.1 %all-gather.3.cloned.1.call-start = ((), (), s32[]{:S(2)}) async-start(), calls=%async_computation | async-start | bytes 2621440 | tf_op jit(solution)/shard_map/all_gather | solution.py:463
  7.9 65.4 %all-gather.5.cloned.1.call-start = ((), (), s32[]{:S(2)}) async-start(), calls=%async_computation.1 | async-start | bytes 2621440 | tf_op jit(solution)/shard_map/all_gather | solution.py:464
  9.6 1.0 %copy-start = (f32[16,4,16,128]{3,2,1,0:T(8,128)S(1)}, f32[16,4,16,128]{3,2,1,0:T(8,128)}, u32[]{:S(2)}) copy-start(f32[16,4,16,128]{3,2,1,0:T(8,128)} %lperm.1) | copy-start | bytes 1572868
  10.6 1.0 %copy-start.2 = (f32[16,4,16,128]{3,2,1,0:T(8,128)S(1)}, f32[16,4,16,128]{3,2,1,0:T(8,128)}, u32[]{:S(2)}) copy-start(f32[16,4,16,128]{3,2,1,0:T(8,128)} %poro.1) | copy-start | bytes 1572868
  11.7 1.2 %copy-start.6 = (f32[16,2,4,16,128]{4,3,2,1,0:T(8,128)S(1)}, f32[16,2,4,16,128]{4,3,2,1,0:T(8,128)}, u32[]{:S(2)}) copy-start(f32[16,2,4,16,128]{4,3,2,1,0:T(8,128)} %rhs.1) | copy-start | bytes 3145732
  12.9 1.0 %copy-start.7 = (f32[16,4,16,128]{3,2,1,0:T(8,128)S(1)}, f32[16,4,16,128]{3,2,1,0:T(8,128)}, u32[]{:S(2)}) copy-start(f32[16,4,16,128]{3,2,1,0:T(8,128)} %sat.1) | copy-start | bytes 1572868
  13.9 1.0 %copy-start.8 = (f32[16,4,16,128]{3,2,1,0:T(8,128)S(1)}, f32[16,4,16,128]{3,2,1,0:T(8,128)}, u32[]{:S(2)}) copy-start(f32[16,4,16,128]{3,2,1,0:T(8,128)} %pres.1) | copy-start | bytes 1572868
  15.0 58.5 %copy-start.9 = (f32[64,256]{1,0:T(8,128)S(1)}, f32[64,256]{1,0:T(8,128)}, u32[]{:S(2)}) copy-start(f32[64,256]{1,0:T(8,128)} %noise.1) | copy-start | bytes 196612
  73.4 1.6 %copy-start.4 = (f32[64,4,16,128]{3,2,1,0:T(8,128)S(1)}, f32[64,4,16,128]{3,2,1,0:T(8,128)}, u32[]{:S(2)}) copy-start(f32[64,4,16,128]{3,2,1,0:T(8,128)} %all-gather.3.cloned.1.call-done) | copy-start | bytes 6291460
  75.0 1.6 %copy-start.5 = (f32[64,4,16,128]{3,2,1,0:T(8,128)S(1)}, f32[64,4,16,128]{3,2,1,0:T(8,128)}, u32[]{:S(2)}) copy-start(f32[64,4,16,128]{3,2,1,0:T(8,128)} %all-gather.5.cloned.1.call-done) | copy-start | bytes 6291460
Sparse Core Ops, SparseCore 0:
  9.6 25.2 all-gather.2
  36.5 22.6 all-gather.4

commit v3 on v2

--- a/solution.py
+++ b/solution.py
@@ -123,8 +123,9 @@
 
 def solve_kernel(
     cell_count, grp_count,
-    rhs, lperm, poro, sat, pres, cells,
-    inc_out, pred_out,
+    rhs_in, lperm_in, poro_in, sat_in, pres_in, cells,
+    inc_hbm, pred_out, all_perm, all_poro,
+    inc_out, inc_sem, rhs, lperm, poro, sat, pres, load_sem, par_send, par_recv,
     powers, tx, gx, ty, gy, tz, gz, halo, gram, gslots, coefs, lhs, pslots, wslots,
     halo_send, halo_recv, gram_send, gram_recv, pick_send, pick_recv, pred_send, pred_recv,
 ):
@@ -134,6 +135,23 @@
     group = members // GROUPS
     has_prev, has_next = me > 0, me < cell_count - 1
 
+    loads = [
+        pltpu.make_async_copy(source, target, load_sem.at[idx])
+        for idx, (source, target) in enumerate(
+            (
+                (lperm_in, lperm),
+                (sat_in, sat),
+                (rhs_in, rhs),
+                (poro_in, poro),
+                (pres_in, pres),
+                (lperm_in, all_perm.at[mine]),
+                (poro_in, all_poro.at[mine]),
+            )
+        )
+    ]
+    for copy in loads:
+        copy.start()
+
     barrier = pltpu.get_barrier_semaphore()
     for step in range(1, cell_count):
         pl.semaphore_signal(
@@ -148,11 +166,11 @@
     def plane(field, part, at):
         part = pl.ds(part * group, group)
         if field == 0:
-            return lperm.at[part, at]
+            return lperm_in.at[part, at]
         if field == 1:
-            return sat.at[part, at]
+            return sat_in.at[part, at]
         if field == 2:
-            return rhs.at[part, 0, at]
+            return rhs_in.at[part, 0, at]
         return powers.at[field - 3, part, 0, at]
 
     def halo_copy(field, part, side):
@@ -186,6 +204,30 @@
     for part in range(GROUPS):
         for field in range(3):
             start_halo(field, part)
+
+    half = grp_count // 2
+    sibling = mine + 1 - 2 * lax.rem(mine, 2)
+
+    def param_copy(which, slot, target, at, relay):
+        everyone = (all_perm, all_poro)[which]
+        own = (lperm_in, poro_in)[which]
+        return pltpu.make_async_remote_copy(
+            src_ref=everyone.at[slot] if relay else own,
+            dst_ref=everyone.at[slot],
+            send_sem=par_send.at[which, at],
+            recv_sem=par_recv.at[which, at],
+            device_id={"grp": target},
+            device_id_type=MESH,
+        )
+
+    params = []
+    for which in range(2):
+        for step in range(1, half):
+            target = lax.rem(mine + 2 * step, grp_count)
+            params.append(param_copy(which, mine, target, step, False))
+        params.append(param_copy(which, mine, sibling, 0, False))
+    for copy in params:
+        copy.start()
 
     @pl.when(me == 0)
     def _():
@@ -224,7 +266,11 @@
                 gx[m, x] = frac
         return carry
 
+    loads[0].wait()
+    loads[1].wait()
     lax.fori_loop(0, members, inner_coeffs, 0)
+    for copy in loads[2:]:
+        copy.wait()
 
     def edge_coeffs(m):
         trans, frac = face_pair(jnp.exp(halo[0, 0, m]), jnp.exp(lperm[m, 0]), halo[0, 1, m], sat[m, 0])
@@ -346,6 +392,13 @@
     mixed = krylov_coefficients([total[:, entry : entry + 1] for entry in range(count)])
     for idx in range(KRYLOV):
         coefs[idx] = jnp.broadcast_to(mixed[idx], (members, cols))
+    for which in range(2):
+        for step in range(1, half):
+            source = lax.rem(mine + grp_count - 2 * step, grp_count)
+            param_copy(which, source, sibling, step, True).wait_recv()
+            copy = param_copy(which, source, sibling, half - 1 + step, True)
+            copy.start()
+            params.append(copy)
 
     def combine(m, carry):
         scale = [coefs[idx, pl.ds(m, 1), :] for idx in range(KRYLOV)]
@@ -362,6 +415,8 @@
         return carry
 
     lax.fori_loop(0, members, combine, 0)
+    store = pltpu.make_async_copy(inc_out, inc_hbm, inc_sem)
+    store.start()
     wells = cells.shape[1] // 2
     for which in range(2):
         cell = cells[:, which * wells : (which + 1) * wells]
@@ -385,8 +440,14 @@
     wslots[mine] = total
     pending += exchange(wslots, mine, grp_count, "grp", pred_send, pred_recv)
     pred_out[...] = wslots[...]
-    for copy in pending:
+    for which in range(2):
+        param_copy(which, sibling, sibling, 0, True).wait_recv()
+        for step in range(1, half):
+            source = lax.rem(sibling + grp_count - 2 * step, grp_count)
+            param_copy(which, source, sibling, half - 1 + step, True).wait_recv()
+    for copy in pending + params:
         copy.wait_send()
+    store.wait()
     for field in range(2 + KRYLOV):
         for part in range(GROUPS):
 
@@ -410,12 +471,28 @@
 
 
 def update_kernel(
-    pred, obs, err, noise, all_perm, all_poro, own_perm, own_poro, perm_out, poro_out
+    pred, obs, err, noise, perm_in, poro_in, own_perm_in, own_poro_in, inc,
+    perm_out, poro_out, inc_out,
+    all_perm, all_poro, own_perm, own_poro, sems,
 ):
+    copies = [
+        pltpu.make_async_copy(source, target, sems.at[idx])
+        for idx, (source, target) in enumerate(
+            (
+                (perm_in, all_perm),
+                (poro_in, all_poro),
+                (own_perm_in, own_perm),
+                (own_poro_in, own_poro),
+                (inc, inc_out),
+            )
+        )
+    ]
+    for copy in copies:
+        copy.start()
     members = pred.shape[0]
-    local_members = own_perm.shape[0]
+    local_members = own_perm_in.shape[0]
     offset = lax.axis_index("grp") * local_members
-    rows, cols = own_perm.shape[1:]
+    rows, cols = own_perm_in.shape[1:]
     sigma = math.sqrt(inflation) * err[...]
     predicted = pred[...]
     center = jnp.sum(predicted, axis=0, keepdims=True) * (1.0 / members)
@@ -439,6 +516,8 @@
     own = dot3(pick, weights, ((1,), (1,))) * (1.0 / math.sqrt(members - 1.0))
     high, middle, _ = split3(own)
     left = jnp.concatenate([high, middle, high], axis=1)
+    for copy in copies[:4]:
+        copy.wait()
     for source, base, out in ((all_perm, own_perm, perm_out), (all_poro, own_poro, poro_out)):
         for row in range(0, rows, 2):
             block = jnp.concatenate([source[:, row, :], source[:, row + 1, :]], axis=1)
@@ -448,6 +527,7 @@
             update = jnp.dot(left, right, preferred_element_type=jnp.float32)
             out[:, row, :] = base[:, row, :] + update[:, :cols]
             out[:, row + 1, :] = base[:, row + 1, :] + update[:, cols:]
+    copies[4].wait()
 
 
 def local(
@@ -460,22 +540,33 @@
     wells = well_cell.shape[0]
     hit = obs_well[:, None] == jnp.arange(wells, dtype=jnp.int32)[None, :]
     cells = jnp.sum(jnp.where(hit, well_cell[None, :], 0), axis=1, dtype=jnp.int32)[None, :]
-    all_perm = lax.all_gather(log_perm, "grp", axis=0, tiled=True)
-    all_poro = lax.all_gather(porosity, "grp", axis=0, tiled=True)
     vmem = pl.BlockSpec(memory_space=pltpu.VMEM)
     f32 = jnp.float32
     field = (members, slab, rows, cols)
     face = (members, slab + 1, rows, cols)
     entries = (KRYLOV + 1) * (KRYLOV + 2) // 2
-    increment, predicted = pl.pallas_call(
+    hbm = pl.BlockSpec(memory_space=pltpu.HBM)
+    increment, predicted, all_perm, all_poro = pl.pallas_call(
         functools.partial(solve_kernel, cell_count, grp_count),
         out_shape=(
             jax.ShapeDtypeStruct(rhs.shape, f32),
             jax.ShapeDtypeStruct((grp_count, members, observations), f32),
+            jax.ShapeDtypeStruct((grp_count,) + field, f32),
+            jax.ShapeDtypeStruct((grp_count,) + field, f32),
         ),
-        in_specs=[vmem] * 6,
-        out_specs=(vmem, vmem),
+        in_specs=[hbm] * 5 + [vmem],
+        out_specs=(hbm, vmem, hbm, hbm),
         scratch_shapes=[
+            pltpu.VMEM(rhs.shape, f32),
+            pltpu.SemaphoreType.DMA,
+            pltpu.VMEM(rhs.shape, f32),
+            pltpu.VMEM(field, f32),
+            pltpu.VMEM(field, f32),
+            pltpu.VMEM(field, f32),
+            pltpu.VMEM(field, f32),
+            pltpu.SemaphoreType.DMA((7,)),
+            pltpu.SemaphoreType.DMA((2, grp_count - 1)),
+            pltpu.SemaphoreType.DMA((2, grp_count - 1)),
             pltpu.VMEM((KRYLOV - 1,) + rhs.shape, f32),
             pltpu.VMEM(face, f32),
             pltpu.VMEM(face, f32),
@@ -500,18 +591,29 @@
             pltpu.SemaphoreType.DMA((grp_count,)),
         ],
         compiler_params=pltpu.CompilerParams(
-            collective_id=0, has_side_effects=True, vmem_limit_bytes=40 * 2**20
+            collective_id=0, has_side_effects=True, vmem_limit_bytes=58 * 2**20
         ),
         cost_estimate=pl.CostEstimate(flops=10**8, bytes_accessed=10**8, transcendentals=0),
     )(rhs, log_perm, porosity, saturation, pressure, cells)
     flat = (members, slab * rows, cols)
     wide = (all_members, slab * rows, cols)
-    perm_post, poro_post = pl.pallas_call(
+    perm_post, poro_post, increment = pl.pallas_call(
         update_kernel,
-        out_shape=(jax.ShapeDtypeStruct(flat, f32), jax.ShapeDtypeStruct(flat, f32)),
-        in_specs=[vmem] * 8,
-        out_specs=(vmem, vmem),
-        compiler_params=pltpu.CompilerParams(vmem_limit_bytes=40 * 2**20),
+        out_shape=(
+            jax.ShapeDtypeStruct(flat, f32),
+            jax.ShapeDtypeStruct(flat, f32),
+            jax.ShapeDtypeStruct(rhs.shape, f32),
+        ),
+        in_specs=[vmem] * 4 + [hbm] * 5,
+        out_specs=(vmem, vmem, hbm),
+        scratch_shapes=[
+            pltpu.VMEM(wide, f32),
+            pltpu.VMEM(wide, f32),
+            pltpu.VMEM(flat, f32),
+            pltpu.VMEM(flat, f32),
+            pltpu.SemaphoreType.DMA((5,)),
+        ],
+        compiler_params=pltpu.CompilerParams(vmem_limit_bytes=60 * 2**20),
     )(
         predicted.reshape(all_members, observations),
         obs_values[None, :],
@@ -521,6 +623,7 @@
         all_poro.reshape(wide),
         log_perm.reshape(flat),
         porosity.reshape(flat),
+        increment,
     )
     return (increment, perm_post.reshape(field), poro_post.reshape(field))
 

time: 95.3 us -> 111 us (1.16)
  Pallas kernels: 68.8 us -> 108 us
  between operations: 14.2 us -> 0.64 us
  local copies, waits for them, and re-layouts: 9.56 us -> 0 us
  waiting for transfers between devices: 1.42 us -> 0 us
    pallas_call x1, Pallas kernels: 10.4 us -> 34.8 us  [local(): pl.pallas_call(update_kernel, out_shape=(jax.ShapeDtypeStruct(flat, f32),...]
    pallas_call x1, Pallas kernels: 58.3 us -> 73.7 us  [local(): pl.pallas_call(functools.partial(solve_kernel, cell_count, grp_count), ou...]
    unnamed x25 -> x0, local copies, waits for them, and re-layouts: 9.56 us -> none
    unnamed x2 -> x0, waiting for transfers between devices: 1.38 us -> none
  transfers between devices with their start and end apart: 2 -> 0, of which waited for: 0 -> 0; matrix products, arithmetic and copies ran while one was open for 1% -> 0% of each run, Pallas kernels for 61% -> 0%
where the time goes in v3:
time: 111 us
  Pallas kernels  108 us (97%)
  other arithmetic  1.44 us (1%)
    pallas_call x1, Pallas kernels, local(): pl.pallas_call(functools.partial(solve_kernel, cell_count, grp_count), ou...  73.7 us
    pallas_call x1, Pallas kernels, local(): pl.pallas_call(update_kernel, out_shape=(jax.ShapeDtypeStruct(flat, f32),...  34.8 us

profile of v3, /device:TPU:0, one launch (start us, length us, event | category | flops | bytes accessed | tf_op | source)
XLA Modules:
  0.0 110.5 jit_solution(1266841014982856746)
XLA Ops:
  0.6 1.4 %select_reduce_fusion = s32[256]{0:T(256)} fusion(s32[128]{0:T(128)} %param.18, s32[256]{0:T(256)} %param.19), kind=kLoop, calls=%fused_computation | loop fusion | flops 98048 | bytes 2560 | tf_op jit(solution)/shard_map/reduce_sum | solution.py:542
  2.1 73.7 %shard_map.121 = (f32[16,2,4,16,128]{4,3,2,1,0:T(8,128)}, f32[4,16,256]{2,1,0:T(8,128)}, f32[4,16,4,16,128]{4,3,2,1,0:T(8,128)}, f32[4,16,4,16,128]{4,3,2,1,0:T(8,128)}) custom-call(f32[16,2,4,16,128]{4,3,2,1,0:T(8,128)} %rhs_in.1, f32[16,4,16,128]{3,2,1,0:T(8,128)} %lperm_in.1, f32[16,4,16,128]{3,2,1,0:T(8,128)} %poro_in.1, f32[16,4,16,128]{3,2,1,0:T(8,128)} %sat_in.1, ...), custom_call_target="tpu_custom_call" | custom-call | flops 100000000 | bytes 100000000 | tf_op jit(solution)/shard_map/pallas_call | solution.py:549
  75.7 34.8 %shard_map.122 = (f32[16,64,128]{2,1,0:T(8,128)}, f32[16,64,128]{2,1,0:T(8,128)}, f32[16,2,4,16,128]{4,3,2,1,0:T(8,128)}) custom-call(f32[64,256]{1,0:T(8,128)} %bitcast.14, f32[1,256]{1,0:T(1,128)} %bitcast.16, f32[1,256]{1,0:T(1,128)} %bitcast.17, f32[64,256]{1,0:T(8,128)} %noise.1, f32[64,64,128]{2,1,0:T(8,128)} %bitcast.10, f32[64,64,128]{2,1,0:T(8,128)} %bitcast.11, ...), custom_call_target="tpu_custom_call" | custom-call | tf_op jit(solution)/shard_map/pallas_call | solution.py:600
